TPU v7x, 32 devices: a whole 2x2x4 slice. The times are simulated.
32 devices in a mesh: dp: 8 (over y, x, core), mp: 4 (over z).
Axes of the slice: x: 2, y: 2, z: 4, core: 2. Of those that a mesh axis runs over, the one named last changes fastest.
Arguments:
- block_in: bfloat16 [2048, 1024], P('dp'), may hold values from -6 to 6
- cotangent: bfloat16 [2048, 1024], P('dp'), may hold values from -6 to 6
- norm_gains: float32 [2, 1024], replicated, may hold values from 0.1 to 1.9
- col_weights: bfloat16 [5, 1024, 1024], P(None, None, 'mp'), may hold values from -0.1875 to 0.1875
- row_weights: bfloat16 [2, 1024, 1024], P(None, 'mp'), may hold values from -0.75 to 0.75
- mem_keys: bfloat16 [2, 4, 256, 128], P(None, 'mp'), may hold values from -0.125 to 0.125
- value_table: bfloat16 [65536, 1024], P(('dp', 'mp')), may hold values from -6 to 6
- col_down: bfloat16 [5, 8, 16, 1024], replicated, may hold values from -0.1875 to 0.1875
- col_up: bfloat16 [5, 8, 16, 1024], P(None, None, None, 'mp'), may hold values from -1.5 to 1.5
- row_down: bfloat16 [2, 8, 16, 1024], P(None, None, None, 'mp'), may hold values from -0.75 to 0.75
- row_up: bfloat16 [2, 8, 16, 1024], replicated, may hold values from -1.5 to 1.5
- segment_ids: int32 [8, 256], P('dp'), may hold values from 0 to 7, never falling along the last dimension, each value on 1 to 128 neighbouring positions
- adapter_ids: int32 [8], P('dp'), may hold values from 0 to 7, as said below
- pick_ids: int32 [2048, 4, 32], P('dp', 'mp'), may hold values from 0 to 65535, as said below
Outputs:
- block_out: bfloat16 [2048, 1024], P('dp')
- input_grad: float32 [2048, 1024], P('dp')
- table_grad: float32 [65536, 1024], P(('dp', 'mp'))
- col_down_grad: float32 [5, 8, 16, 1024], replicated
- col_up_grad: float32 [5, 8, 16, 1024], P(None, None, None, 'mp')
- row_down_grad: float32 [2, 8, 16, 1024], P(None, None, None, 'mp')
- row_up_grad: float32 [2, 8, 16, 1024], replicated
Inputs may be any that keep to these rules, and one draw needn't show every extreme that they name: `pick_ids`: owner o, the device whose index over dp+mp is o, holds rows o * 2048 to (o + 1) * 2048 - 1. Among the picks of one memory head for one aligned block of 128 tokens of a sequence at most 256 lie in one owner's rows, and in every such block the same quarter of the owners holds exactly 256. `adapter_ids`: every adapter is named by exactly 1 sequence. `segment_ids`: along a sequence the document number never falls; a document holds at most 128 tokens, and one holds exactly that many.
All inputs are finite; a program needn't handle non-finite values.
Results may differ from a plain program's by a relative error of at most 0.018.
Values may be sent and summed in bfloat16 or wider, within the bound.
A program may use at most 192 MiB of HBM per device.

v0:
```python
import jax
import jax.numpy as jnp
from jax import lax
from jax.sharding import PartitionSpec as P

HEAD_DIM = 64
MEM_BLK = 128


EPSILON = 1e-05
ADAPT_SCALE = 0.5


def matmul(left, right):
    return jnp.dot(left, right, preferred_element_type=jnp.float32)


def matmul_nt(left, right):
    return lax.dot_general(
        left, right, (((1,), (1,)), ((), ())), preferred_element_type=jnp.float32
    )


def matmul_tn(left, right):
    return lax.dot_general(
        left, right, (((0,), (0,)), ((), ())), preferred_element_type=jnp.float32
    )


def rms_scale(values):
    return lax.rsqrt(jnp.mean(values * values, axis=-1, keepdims=True) + EPSILON)


def silu_slope(gate):
    sigma = jax.nn.sigmoid(gate)
    return sigma * (1.0 + gate * (1.0 - sigma))


def pick_scores(pick_blk, first_blk, second_blk, sub_count):
    columns = jnp.arange(sub_count, dtype=jnp.int32)
    hit_first = (pick_blk // sub_count)[:, :, None] == columns
    hit_second = (pick_blk % sub_count)[:, :, None] == columns
    scores = jnp.sum(jnp.where(hit_first, first_blk[:, None, :], 0.0), axis=2)
    scores = scores + jnp.sum(jnp.where(hit_second, second_blk[:, None, :], 0.0), axis=2)
    return (jax.nn.softmax(scores, axis=-1), hit_first, hit_second)


def slot_places(pick_blk, rows_here, owners):
    flat = pick_blk.reshape(-1)
    owner_id = flat // rows_here
    local_row = flat % rows_here
    owner_hits = (owner_id[:, None] == jnp.arange(owners, dtype=jnp.int32)).astype(jnp.int32)
    before = jnp.cumsum(owner_hits, axis=0) - owner_hits
    slot_rank = jnp.sum(before * owner_hits, axis=1)
    return (owner_id, local_row, slot_rank)


def per_device(
    block_in,
    cotangent,
    norm_gains,
    col_weights,
    row_weights,
    mem_keys,
    value_table,
    col_down,
    col_up,
    row_down,
    row_up,
    segment_ids,
    adapter_ids,
    pick_ids,
):
    floating = jnp.float32
    brain = jnp.bfloat16
    length, width = block_in.shape
    col_width = col_weights.shape[2]
    heads_here = col_width // HEAD_DIM
    owners = lax.axis_size("dp") * lax.axis_size("mp")
    rows_here = value_table.shape[0]
    pick_tok = pick_ids[:, 0, :]
    pick_count = pick_tok.shape[1]
    num_blocks = length // MEM_BLK
    capacity = 2 * MEM_BLK * pick_count // owners
    query_rows = min(512, length)
    query_blocks = length // query_rows
    sub_count = mem_keys.shape[2]
    half_width = mem_keys.shape[3]
    adapter = adapter_ids[0]
    down_col = lax.dynamic_index_in_dim(col_down, adapter, 1, keepdims=False)
    up_col = lax.dynamic_index_in_dim(col_up, adapter, 1, keepdims=False)
    down_row = lax.dynamic_index_in_dim(row_down, adapter, 1, keepdims=False)
    up_row = lax.dynamic_index_in_dim(row_up, adapter, 1, keepdims=False)
    gain_one = norm_gains[0]
    gain_two = norm_gains[1]
    first_keys = mem_keys[0, 0]
    second_keys = mem_keys[1, 0]
    segments = segment_ids[0]
    positions = jnp.arange(length, dtype=jnp.int32)
    inputs = block_in.astype(floating)
    scale_one = rms_scale(inputs)
    normed_one = (inputs * scale_one * gain_one).astype(brain)
    low_att = jnp.einsum(
        "td,jrd->jtr", normed_one, down_col[:3], preferred_element_type=floating
    ).astype(brain)
    projected = jnp.einsum(
        "td,jde->jte", normed_one, col_weights[:3], preferred_element_type=floating
    )
    projected = projected + ADAPT_SCALE * jnp.einsum(
        "jtr,jre->jte", low_att, up_col[:3], preferred_element_type=floating
    )
    projected = projected.astype(brain)
    queries = projected[0].reshape(length, heads_here, HEAD_DIM)
    keys_here = projected[1].reshape(length, heads_here, HEAD_DIM)
    values_here = projected[2].reshape(length, heads_here, HEAD_DIM)

    def block_logits(start):
        rows_pos = start + jnp.arange(query_rows, dtype=jnp.int32)
        allowed = (segments[:, None] == segments[None, :]) & (
            positions[None, :] <= rows_pos[:, None]
        )
        logits = (
            jnp.einsum("thd,shd->hts", queries, keys_here, preferred_element_type=floating) * 0.125
        )
        return (queries, allowed, jnp.where(allowed[None], logits, -1e30))

    def attend(index):
        query_blk, allowed, logits = block_logits(index * query_rows)
        peak = jnp.max(logits, axis=-1, keepdims=True)
        expos = jnp.exp(logits - peak)
        total = jnp.sum(expos, axis=-1, keepdims=True)
        probs = expos / total
        mixed = jnp.einsum(
            "hts,shd->thd", probs.astype(brain), values_here, preferred_element_type=floating
        )
        return (
            mixed.reshape(query_rows, col_width).astype(brain),
            (peak + jnp.log(total))[:, :, 0],
        )

    att_out, log_totals = lax.map(attend, jnp.arange(query_blocks))
    att_out = att_out.reshape(length, col_width)
    att_part = matmul(att_out, row_weights[0])
    low_part = matmul_nt(att_out, down_row[0])
    att_sum, low_sum = lax.psum((att_part, low_part), "mp")
    low_out = low_sum.astype(brain)
    resid = inputs + att_sum + ADAPT_SCALE * matmul(low_out, up_row[0])
    scale_two = rms_scale(resid)
    normed_two = (resid * scale_two * gain_two).astype(brain)
    low_mem = jnp.einsum(
        "td,jrd->jtr", normed_two, down_col[3:], preferred_element_type=floating
    ).astype(brain)
    mem_query = (
        matmul(normed_two, col_weights[3]) + ADAPT_SCALE * matmul(low_mem[0], up_col[3])
    ).astype(brain)
    gate_pre = matmul(normed_two, col_weights[4]) + ADAPT_SCALE * matmul(low_mem[1], up_col[4])
    first_sub = matmul_nt(mem_query[:, :half_width], first_keys)
    second_sub = matmul_nt(mem_query[:, half_width:], second_keys)

    def block_inputs(index):
        start = index * MEM_BLK
        pick_blk = lax.dynamic_slice_in_dim(pick_tok, start, MEM_BLK, 0)
        first_blk = lax.dynamic_slice_in_dim(first_sub, start, MEM_BLK, 0)
        second_blk = lax.dynamic_slice_in_dim(second_sub, start, MEM_BLK, 0)
        return (pick_blk, first_blk, second_blk)

    def gather_rows(index):
        pick_blk, first_blk, second_blk = block_inputs(index)
        weights_blk, hit_first, hit_second = pick_scores(pick_blk, first_blk, second_blk, sub_count)
        owner_id, local_row, slot_rank = slot_places(pick_blk, rows_here, owners)
        requests = (
            jnp.full((owners, capacity), -1, jnp.int32).at[owner_id, slot_rank].set(local_row)
        )
        arrived = lax.all_to_all(requests, ("dp", "mp"), split_axis=0, concat_axis=0, tiled=True)
        fetched = value_table[jnp.maximum(arrived, 0)]
        returned = lax.all_to_all(fetched, ("dp", "mp"), split_axis=0, concat_axis=0, tiled=True)
        picked = returned[owner_id, slot_rank].reshape(MEM_BLK, pick_count, width)
        memory = jnp.einsum(
            "tp,tpd->td", weights_blk.astype(brain), picked, preferred_element_type=floating
        )
        kept_rows = jnp.zeros((1, 1, 1), brain)
        return (memory, arrived, kept_rows)

    memory, arrivals, kept_all = lax.map(gather_rows, jnp.arange(num_blocks))
    mem_cols = lax.psum_scatter(
        memory.reshape(length, width), "mp", scatter_dimension=1, tiled=True
    )
    gate_act = jax.nn.silu(gate_pre)
    gated = (mem_cols * gate_act).astype(brain)
    branch_part = matmul(gated, row_weights[1])
    low_branch_part = matmul_nt(gated, down_row[1])
    branch_sum, low_branch_sum = (
        lax.psum(branch_part.astype(jnp.bfloat16), "mp").astype(jnp.float32),
        lax.psum(low_branch_part.astype(jnp.bfloat16), "mp").astype(jnp.float32),
    )
    low_branch = low_branch_sum.astype(brain)
    block_out = (resid + branch_sum + ADAPT_SCALE * matmul(low_branch, up_row[1])).astype(brain)
    out_grad = cotangent.astype(floating)
    low_branch_grad = (ADAPT_SCALE * matmul_nt(cotangent, up_row[1])).astype(brain)
    grad_up_branch = ADAPT_SCALE * matmul_tn(low_branch, cotangent)
    gated_grad = matmul_nt(cotangent, row_weights[1]) + matmul(low_branch_grad, down_row[1])
    grad_down_branch = matmul_tn(low_branch_grad, gated)
    mem_grad_cols = (gated_grad * gate_act).astype(brain)
    gate_grad = (gated_grad * mem_cols * silu_slope(gate_pre)).astype(brain)
    mem_grad = lax.all_gather(mem_grad_cols, "mp", axis=1, tiled=True)

    def scatter_back(table_acc, index):
        pick_blk, first_blk, second_blk = block_inputs(index)
        grad_blk = lax.dynamic_slice_in_dim(mem_grad, index * MEM_BLK, MEM_BLK, 0)
        weights_blk, hit_first, hit_second = pick_scores(pick_blk, first_blk, second_blk, sub_count)
        owner_id, local_row, slot_rank = slot_places(pick_blk, rows_here, owners)
        token_of = jnp.arange(MEM_BLK * pick_count, dtype=jnp.int32) // pick_count
        send_grads = (
            jnp.zeros((owners, capacity, width), brain)
            .at[owner_id, slot_rank]
            .set(grad_blk[token_of])
        )
        send_weights = (
            jnp.zeros((owners, capacity), brain)
            .at[owner_id, slot_rank]
            .set(weights_blk.astype(brain).reshape(-1))
        )
        got_grads, got_weights = (
            lax.all_to_all(send_grads, ("dp", "mp"), split_axis=0, concat_axis=0, tiled=True),
            lax.all_to_all(send_weights, ("dp", "mp"), split_axis=0, concat_axis=0, tiled=True),
        )
        safe_rows = jnp.maximum(arrivals[index], 0)
        contrib = got_grads.astype(floating) * got_weights.astype(floating)[:, :, None]
        table_acc = table_acc.at[safe_rows.reshape(-1)].add(contrib.reshape(-1, width))
        products = jnp.einsum(
            "scd,scd->sc", value_table[safe_rows], got_grads, preferred_element_type=floating
        )
        answered = lax.all_to_all(products, ("dp", "mp"), split_axis=0, concat_axis=0, tiled=True)
        weight_grad = answered[owner_id, slot_rank].reshape(MEM_BLK, pick_count)
        score_grad = weights_blk * (
            weight_grad - jnp.sum(weights_blk * weight_grad, axis=-1, keepdims=True)
        )
        first_grad = jnp.sum(jnp.where(hit_first, score_grad[:, :, None], 0.0), axis=1).astype(
            brain
        )
        second_grad = jnp.sum(jnp.where(hit_second, score_grad[:, :, None], 0.0), axis=1).astype(
            brain
        )
        query_grad = jnp.concatenate(
            [matmul(first_grad, first_keys), matmul(second_grad, second_keys)], axis=1
        ).astype(brain)
        return (table_acc, query_grad)

    table_grad, query_grads = lax.scan(
        scatter_back, jnp.zeros((rows_here, width), floating), jnp.arange(num_blocks)
    )
    query_grad = query_grads.reshape(length, col_width)
    normed_two_part = matmul_nt(query_grad, col_weights[3]) + matmul_nt(gate_grad, col_weights[4])
    low_mem_part = ADAPT_SCALE * jnp.stack(
        [matmul_nt(query_grad, up_col[3]), matmul_nt(gate_grad, up_col[4])]
    )
    grad_up_mem = ADAPT_SCALE * jnp.stack(
        [matmul_tn(low_mem[0], query_grad), matmul_tn(low_mem[1], gate_grad)]
    )
    normed_two_grad, low_mem_grad = lax.psum((normed_two_part, low_mem_part), "mp")
    low_mem_grad = low_mem_grad.astype(brain)
    normed_two_grad = normed_two_grad + jnp.einsum(
        "jtr,jrd->td", low_mem_grad, down_col[3:], preferred_element_type=floating
    )
    grad_down_mem = jnp.einsum(
        "jtr,td->jrd", low_mem_grad, normed_two, preferred_element_type=floating
    )
    weighted_two = gain_two * normed_two_grad
    resid_grad = (
        out_grad
        + scale_two * weighted_two
        - resid * scale_two**3 * jnp.mean(resid * weighted_two, axis=-1, keepdims=True)
    )
    att_branch_grad = resid_grad.astype(brain)
    low_out_grad = (ADAPT_SCALE * matmul_nt(att_branch_grad, up_row[0])).astype(brain)
    grad_up_att = ADAPT_SCALE * matmul_tn(low_out, att_branch_grad)
    att_out_grad = (
        matmul_nt(att_branch_grad, row_weights[0]) + matmul(low_out_grad, down_row[0])
    ).astype(brain)
    grad_down_att = matmul_tn(low_out_grad, att_out)

    def attend_back(carry, index):
        key_acc, value_acc = carry
        start = index * query_rows
        query_blk, allowed, logits = block_logits(start)
        grad_blk = att_out_grad.reshape(query_rows, heads_here, HEAD_DIM)
        probs = jnp.where(allowed[None], jnp.exp(logits - log_totals[index][:, :, None]), 0.0)
        value_acc = value_acc + jnp.einsum(
            "hts,thd->shd", probs.astype(brain), grad_blk, preferred_element_type=floating
        )
        prob_grad = jnp.einsum(
            "thd,shd->hts", grad_blk, values_here, preferred_element_type=floating
        )
        logit_grad = (
            probs * (prob_grad - jnp.sum(probs * prob_grad, axis=-1, keepdims=True))
        ).astype(brain)
        query_part = 0.125 * jnp.einsum(
            "hts,shd->thd", logit_grad, keys_here, preferred_element_type=floating
        )
        key_acc = key_acc + 0.125 * jnp.einsum(
            "hts,thd->shd", logit_grad, query_blk, preferred_element_type=floating
        )
        return ((key_acc, value_acc), query_part.reshape(query_rows, col_width).astype(brain))

    empty = jnp.zeros((length, heads_here, HEAD_DIM), floating)
    (key_grad, value_grad), query_parts = lax.scan(
        attend_back, (empty, empty), jnp.arange(query_blocks)
    )
    proj_grad = jnp.stack(
        [
            query_parts.reshape(length, col_width),
            key_grad.reshape(length, col_width).astype(brain),
            value_grad.reshape(length, col_width).astype(brain),
        ]
    )
    normed_one_part = jnp.einsum(
        "jte,jde->td", proj_grad, col_weights[:3], preferred_element_type=floating
    )
    low_att_part = ADAPT_SCALE * jnp.einsum(
        "jte,jre->jtr", proj_grad, up_col[:3], preferred_element_type=floating
    )
    grad_up_qkv = ADAPT_SCALE * jnp.einsum(
        "jtr,jte->jre", low_att, proj_grad, preferred_element_type=floating
    )
    normed_one_grad, low_att_grad = (
        lax.psum(normed_one_part.astype(jnp.bfloat16), "mp").astype(jnp.float32),
        lax.psum(low_att_part.astype(jnp.bfloat16), "mp").astype(jnp.float32),
    )
    low_att_grad = low_att_grad.astype(brain)
    normed_one_grad = normed_one_grad + jnp.einsum(
        "jtr,jrd->td", low_att_grad, down_col[:3], preferred_element_type=floating
    )
    grad_down_qkv = jnp.einsum(
        "jtr,td->jrd", low_att_grad, normed_one, preferred_element_type=floating
    )
    weighted_one = gain_one * normed_one_grad
    input_grad = (
        resid_grad
        + scale_one * weighted_one
        - inputs * scale_one**3 * jnp.mean(inputs * weighted_one, axis=-1, keepdims=True)
    )
    chosen = (jnp.arange(col_down.shape[1], dtype=jnp.int32) == adapter).astype(floating)
    down_cols_all = (
        jnp.concatenate([grad_down_qkv, grad_down_mem], axis=0)[:, None]
        * chosen[None, :, None, None]
    )
    up_cols_all = (
        jnp.concatenate([grad_up_qkv, grad_up_mem], axis=0)[:, None] * chosen[None, :, None, None]
    )
    down_rows_all = (
        jnp.stack([grad_down_att, grad_down_branch])[:, None] * chosen[None, :, None, None]
    )
    up_rows_all = jnp.stack([grad_up_att, grad_up_branch])[:, None] * chosen[None, :, None, None]
    down_cols_sum, up_cols_sum, down_rows_sum, up_rows_sum = (
        lax.psum(down_cols_all.astype(jnp.bfloat16), "dp").astype(jnp.float32),
        lax.psum(up_cols_all.astype(jnp.bfloat16), "dp").astype(jnp.float32),
        lax.psum(down_rows_all.astype(jnp.bfloat16), "dp").astype(jnp.float32),
        lax.psum(up_rows_all.astype(jnp.bfloat16), "dp").astype(jnp.float32),
    )
    return (
        block_out,
        input_grad,
        table_grad,
        down_cols_sum,
        up_cols_sum,
        down_rows_sum,
        up_rows_sum,
    )


def solution(mesh):
    in_specs = (
        P("dp", None),
        P("dp", None),
        P(),
        P(None, None, "mp"),
        P(None, "mp", None),
        P(None, "mp", None, None),
        P(("dp", "mp"), None),
        P(),
        P(None, None, None, "mp"),
        P(None, None, None, "mp"),
        P(),
        P("dp", None),
        P("dp"),
        P("dp", "mp", None),
    )
    out_specs = (
        P("dp", None),
        P("dp", None),
        P(("dp", "mp"), None),
        P(),
        P(None, None, None, "mp"),
        P(None, None, None, "mp"),
        P(),
    )
    return jax.shard_map(
        per_device, mesh=mesh, in_specs=in_specs, out_specs=out_specs, check_vma=False
    )
```

profile of v0, /device:TPU:0, one launch (start us, length us, event | category | flops | bytes accessed | tf_op | source)
XLA Modules:
  0.0 2788.0 jit_solution(10000760891726592531)
XLA Ops:
  42.2 32.2 %all-reduce.8.cloned.1.call-done = f32[256,1024]{1,0:T(8,128)} async-done(((f32[256,1024]{1,0:T(8,128)}), f32[256,1024]{1,0:T(8,128)}) %all-reduce.8.cloned.1.call-update) | async-done | bytes 1048592 | tf_op jit(solution)/shard_map/psum | solution.py:145
  80.4 1086.1 %while.20 = (s32[]{:T(128)}, f32[2,128,1024]{2,1,0:T(8,128)}, s32[2,32,256]{2,0,1:T(2,128)}, s32[2]{0:T(128)S(1)}, s32[256,32]{1,0:T(8,128)S(1)}, /*index=5*/f32...) while((s32[]{:T(128)}, f32[2,128,1024]{2,1,0:T(8,128)}, ...), condition=%wide.region_15.16_spmd, body=%wide.region_6.0_spmd.sunk | while | flops 32853732 | bytes 124878008 | solution.py:184
  122.7 43.4 %gather_fusion = bf16[8192,1024]{1,0:T(8,128)(2,1)} fusion(bf16[2048,1024]{1,0:T(8,128)(2,1)} %get-tuple-element.761, s32[8192]{0:T(1024)S(1)} %broadcast_clamp_fusion.6), kind=kCustom, calls=%fused_computation.clone.1 | custom fusion | bytes 33587200 | tf_op jit(solution)/shard_map/while/body/eval_jaxpr/gather | solution.py:175
  179.3 351.0 %all-to-all-done.1 = bf16[32,256,1024]{2,1,0:T(8,128)(2,1)} async-done(((bf16[32,256,1024]{2,1,0:T(8,128)(2,1)}), bf16[32,256,1024]{2,1,0:T(8,128)(2,1)}, u32[]{:S(2)}, u32[]{:S(2)}) %all-to-all-start.1) | async-done | bytes 16777248 | tf_op jit(solution)/shard_map/while/body/eval_jaxpr/all_to_all | solution.py:176
  530.3 81.2 %gather_fusion.1 = bf16[4096,1024]{1,0:T(8,128)(2,1)} fusion(bf16[32,256,1024]{2,1,0:T(8,128)(2,1)} %all-to-all-done.1, s32[4096]{0:T(1024)S(1)} %bitcast.356), kind=kCustom, calls=%fused_computation.1.clone.1 | custom fusion | bytes 16809984 | tf_op jit(solution)/shard_map/while/body/eval_jaxpr/gather | solution.py:177
  671.6 43.4 %gather_fusion = bf16[8192,1024]{1,0:T(8,128)(2,1)} fusion(bf16[2048,1024]{1,0:T(8,128)(2,1)} %get-tuple-element.761, s32[8192]{0:T(1024)S(1)} %broadcast_clamp_fusion.6), kind=kCustom, calls=%fused_computation.clone.1 | custom fusion | bytes 33587200 | tf_op jit(solution)/shard_map/while/body/eval_jaxpr/gather | solution.py:175
  728.2 351.0 %all-to-all-done.1 = bf16[32,256,1024]{2,1,0:T(8,128)(2,1)} async-done(((bf16[32,256,1024]{2,1,0:T(8,128)(2,1)}), bf16[32,256,1024]{2,1,0:T(8,128)(2,1)}, u32[]{:S(2)}, u32[]{:S(2)}) %all-to-all-start.1) | async-done | bytes 16777248 | tf_op jit(solution)/shard_map/while/body/eval_jaxpr/all_to_all | solution.py:176
  1079.2 81.5 %gather_fusion.1 = bf16[4096,1024]{1,0:T(8,128)(2,1)} fusion(bf16[32,256,1024]{2,1,0:T(8,128)(2,1)} %all-to-all-done.1, s32[4096]{0:T(1024)S(1)} %bitcast.356), kind=kCustom, calls=%fused_computation.1.clone.1 | custom fusion | bytes 16809984 | tf_op jit(solution)/shard_map/while/body/eval_jaxpr/gather | solution.py:177
  1175.2 29.3 %reduce-scatter.2.cloned.1.call-done = f32[256,256]{1,0:T(8,128)} async-done(((f32[256,1024]{1,0:T(8,128)}), f32[256,256]{1,0:T(8,128)}) %reduce-scatter.2.cloned.1.call-update) | async-done | bytes 262160 | tf_op jit(solution)/shard_map/reduce_scatter | solution.py:185
  1228.0 1304.6 %while.42 = (s32[]{:T(128)}, f32[2048,1024]{1,0:T(8,128)}, bf16[2,128,256]{2,1,0:T(8,128)(2,1)}, s32[2]{0:T(128)}, s32[2,32,256]{2,0,1:T(2,128)}, /*index=5*/s32...) while((s32[]{:T(128)}, f32[2048,1024]{1,0:T(8,128)}, ...), condition=%wide.region_33.34_spmd, body=%wide.region_19.33_spmd.sunk | while | flops 98020968 | bytes 284183424 | solution.py:249
  1272.5 28.6 %scatter_custom_fusion.18 = bf16[8192]{0:T(1024)(128)(2,1)S(1)} fusion(s32[4096]{0:T(1024)S(1)} %get-tuple-element.712, bf16[4096]{0:T(1024)(128)(2,1)S(1)} %reshape.996, bf16[]{:T(256)} %constant.370.clone.1..sunk), kind=kCustom, calls=%fused_computation.144.clone.1 | custom fusion | bytes 16386 | tf_op jit(solution)/shard_map/while
  1305.9 57.4 %scatter_custom_fusion.19 = bf16[8192,1024]{1,0:T(8,128)(2,1)} fusion(s32[4096]{0:T(1024)S(1)} %get-tuple-element.712, bf16[128,1024]{1,0:T(8,128)(2,1)S(1)} %constant_dynamic-slice_fusion.17, s32[4096]{0:T(1024)S(1)} %get-tuple-element.718, bf16[]{:T(256)} %constant.370.clone.1..sunk), kind=kCustom, calls=%fused_computation.71.clone.1 | custom fusion | bytes 16777218 | tf_op jit(solution)/shard_map/while
  1372.1 43.4 %gather_fusion.2 = bf16[8192,1024]{1,0:T(8,128)(2,1)} fusion(bf16[2048,1024]{1,0:T(8,128)(2,1)} %get-tuple-element.820, s32[8192]{0:T(1024)S(1)} %broadcast_clamp_fusion.8), kind=kCustom, calls=%fused_computation.3.clone.1 | custom fusion | bytes 33587200 | tf_op jit(solution)/shard_map/while/body/eval_jaxpr/gather | solution.py:231
  1415.5 313.9 %all-to-all-done.3 = bf16[32,256,1024]{2,1,0:T(8,128)(2,1)} async-done(((bf16[32,256,1024]{2,1,0:T(8,128)(2,1)}), bf16[32,256,1024]{2,1,0:T(8,128)(2,1)}, u32[]{:S(2)}, u32[]{:S(2)}) %all-to-all-start.3) | async-done | bytes 16777248 | tf_op jit(solution)/shard_map/while/body/eval_jaxpr/all_to_all | solution.py:224
  1770.7 77.7 %scatter_fusion = f32[2048,1024]{1,0:T(8,128)} fusion(f32[2048,1024]{1,0:T(8,128)} %get-tuple-element.791, s32[8192]{0:T(1024)S(1)} %bitcast.366, f32[8192,1024]{1,0:T(8,128)} %bitcast.358), kind=kCustom, calls=%fused_computation.6.clone.1 | custom fusion | flops 8388608 | bytes 100696064 | tf_op jit(solution)/shard_map/while/body/eval_jaxpr/scatter-add | solution.py:229
  1849.3 32.8 %gather_fusion.3 = f32[4096]{0:T(1024)S(1)} fusion(f32[32,256]{1,0:T(8,128)S(1)} %bitcast.355, s32[4096]{0:T(1024)S(1)} %bitcast.357), kind=kCustom, calls=%fused_computation.4.clone.1 | custom fusion | bytes 65536 | tf_op jit(solution)/shard_map/while/body/eval_jaxpr/gather | solution.py:234
  1946.7 57.4 %scatter_custom_fusion.19 = bf16[8192,1024]{1,0:T(8,128)(2,1)} fusion(s32[4096]{0:T(1024)S(1)} %get-tuple-element.712, bf16[128,1024]{1,0:T(8,128)(2,1)S(1)} %constant_dynamic-slice_fusion.17, s32[4096]{0:T(1024)S(1)} %get-tuple-element.718, bf16[]{:T(256)} %constant.370.clone.1..sunk), kind=kCustom, calls=%fused_computation.71.clone.1 | custom fusion | bytes 16777218 | tf_op jit(solution)/shard_map/while
  2012.9 43.4 %gather_fusion.2 = bf16[8192,1024]{1,0:T(8,128)(2,1)} fusion(bf16[2048,1024]{1,0:T(8,128)(2,1)} %get-tuple-element.820, s32[8192]{0:T(1024)S(1)} %broadcast_clamp_fusion.8), kind=kCustom, calls=%fused_computation.3.clone.1 | custom fusion | bytes 33587200 | tf_op jit(solution)/shard_map/while/body/eval_jaxpr/gather | solution.py:231
  2056.3 313.9 %all-to-all-done.3 = bf16[32,256,1024]{2,1,0:T(8,128)(2,1)} async-done(((bf16[32,256,1024]{2,1,0:T(8,128)(2,1)}), bf16[32,256,1024]{2,1,0:T(8,128)(2,1)}, u32[]{:S(2)}, u32[]{:S(2)}) %all-to-all-start.3) | async-done | bytes 16777248 | tf_op jit(solution)/shard_map/while/body/eval_jaxpr/all_to_all | solution.py:224
  2411.5 77.7 %scatter_fusion = f32[2048,1024]{1,0:T(8,128)} fusion(f32[2048,1024]{1,0:T(8,128)} %get-tuple-element.791, s32[8192]{0:T(1024)S(1)} %bitcast.366, f32[8192,1024]{1,0:T(8,128)} %bitcast.358), kind=kCustom, calls=%fused_computation.6.clone.1 | custom fusion | flops 8388608 | bytes 100696064 | tf_op jit(solution)/shard_map/while/body/eval_jaxpr/scatter-add | solution.py:229
  2490.1 32.8 %gather_fusion.3 = f32[4096]{0:T(1024)S(1)} fusion(f32[32,256]{1,0:T(8,128)S(1)} %bitcast.355, s32[4096]{0:T(1024)S(1)} %bitcast.357), kind=kCustom, calls=%fused_computation.4.clone.1 | custom fusion | bytes 65536 | tf_op jit(solution)/shard_map/while/body/eval_jaxpr/gather | solution.py:234
  2565.9 44.7 %all-reduce.10.cloned.1.call-done = f32[256,1024]{1,0:T(8,128)} async-done(((f32[256,1024]{1,0:T(8,128)}), f32[256,1024]{1,0:T(8,128)}) %all-reduce.10.cloned.1.call-update) | async-done | bytes 1048592 | tf_op jit(solution)/shard_map/psum | solution.py:260
  2666.5 42.2 %all-reduce.14.cloned.1.call-done = (bf16[256,1024]{1,0:T(8,128)(2,1)}, bf16[256,1024]{1,0:T(8,128)(2,1)}) async-done(((bf16[256,1024]{1,0:T(8,128)(2,1)}, bf16[256,1024]{1,0:T(8,128)(2,1)}), (bf16[256,1024]{1,0:T(8,128)(2,1)}, bf16[256,1024]{1,0:T(8,128)(2,1)})) %all-reduce.14.cloned.1.call-update) | async-done | bytes 1048592 | tf_op jit(solution)/shard_map/psum | solution.py:193
  2713.9 61.4 %all-reduce.12.cloned.1.call-done = (bf16[5,8,16,1024]{3,2,1,0:T(8,128)(2,1)}, bf16[5,8,16,256]{3,2,1,0:T(8,128)(2,1)}, bf16[2,8,16,256]{3,2,1,0:T(8,128)(2,1)}, bf16[2,8,16,1024]{3,2,1,0:T(8,128)(2,1)}) async-done(((bf16[5,8,16,1024]{3,2,1,0:T(8,128)(2,1)}, bf16[5,8,16,256]{3,2,1,0:T(8,128)(2,1)}, bf16[2,8,16,256]{3,2,1,0:T(8,128)(2,1)}, bf16[2,8,16,1024]{3,2,1,0:T(8,128)(2,1)}), ...) | async-done | bytes 2293776 | tf_op jit(solution)/shard_map/psum | solution.py:355
  (514 shorter events, 498.7 us)
Async XLA Ops:
  7.2 67.2 %all-reduce.8.cloned.1.call-start = ((), (), s32[]{:S(2)}) async-start(), calls=%async_computation.6 | async-start | bytes 2097152 | tf_op jit(solution)/shard_map/psum | solution.py:145
  19.4 1185.1 %reduce-scatter.2.cloned.1.call-start = ((), (), s32[]{:S(2)}) async-start(), calls=%async_computation.7 | async-start | bytes 1310720 | tf_op jit(solution)/shard_map/reduce_scatter | solution.py:185
  80.4 1093.4 %copy-start.13 = (bf16[256,1024]{1,0:T(8,128)(2,1)S(1)}, bf16[256,1024]{1,0:T(8,128)(2,1)}, u32[]{:S(2)}) copy-start(bf16[256,1024]{1,0:T(8,128)(2,1)} %copy-done.12) | copy-start | bytes 1572868
  166.1 364.2 %all-to-all-start.1 = ((bf16[32,256,1024]{2,1,0:T(8,128)(2,1)}), bf16[32,256,1024]{2,1,0:T(8,128)(2,1)}, u32[]{:S(2)}, u32[]{:S(2)}) async-start(bf16[32,256,1024]{2,1,0:T(8,128)(2,1)} %bitcast.361), calls=%async_computation.1 | async-start | bytes 33554432 | tf_op jit(solution)/shard_map/while/body/eval_jaxpr/all_to_all | solution.py:176
  179.3 432.2 %copy-start.49 = (s32[2,32,256]{2,0,1:T(2,128)}, s32[2,32,256]{2,0,1:T(2,128)S(1)}, u32[]{:S(2)}) copy-start(s32[2,32,256]{2,0,1:T(2,128)S(1)} %dynamic_update_slice.38) | copy-start | bytes 196612 | tf_op jit(solution)/shard_map/while
  715.0 364.2 %all-to-all-start.1 = ((bf16[32,256,1024]{2,1,0:T(8,128)(2,1)}), bf16[32,256,1024]{2,1,0:T(8,128)(2,1)}, u32[]{:S(2)}, u32[]{:S(2)}) async-start(bf16[32,256,1024]{2,1,0:T(8,128)(2,1)} %bitcast.361), calls=%async_computation.1 | async-start | bytes 33554432 | tf_op jit(solution)/shard_map/while/body/eval_jaxpr/all_to_all | solution.py:176
  728.2 432.5 %copy-start.49 = (s32[2,32,256]{2,0,1:T(2,128)}, s32[2,32,256]{2,0,1:T(2,128)S(1)}, u32[]{:S(2)}) copy-start(s32[2,32,256]{2,0,1:T(2,128)S(1)} %dynamic_update_slice.38) | copy-start | bytes 196612 | tf_op jit(solution)/shard_map/while
  1166.6 1444.1 %all-reduce.10.cloned.1.call-start = ((), (), s32[]{:S(2)}) async-start(), calls=%async_computation.8 | async-start | bytes 2097152 | tf_op jit(solution)/shard_map/psum | solution.py:260
  1228.0 1308.3 %copy-start.58 = (bf16[2,256,16]{1,2,0:T(8,128)(2,1)S(1)}, bf16[2,256,16]{1,2,0:T(8,128)(2,1)}, u32[]{:S(2)}) copy-start(bf16[2,256,16]{1,2,0:T(8,128)(2,1)} %copy-done.56) | copy-start | bytes 49156
  1248.4 114.9 %copy-start.15 = (f32[256,256]{1,0:T(8,128)}, f32[256,256]{1,0:T(8,128)S(1)}, u32[]{:S(2)}) copy-start(f32[256,256]{1,0:T(8,128)S(1)} %get-tuple-element.819) | copy-start | bytes 786436 | tf_op jit(solution)/shard_map/while
  1248.4 114.9 %copy-start.17 = (f32[256,256]{1,0:T(8,128)}, f32[256,256]{1,0:T(8,128)S(1)}, u32[]{:S(2)}) copy-start(f32[256,256]{1,0:T(8,128)S(1)} %get-tuple-element.818) | copy-start | bytes 786436 | tf_op jit(solution)/shard_map/while
  1250.3 112.9 %copy-start.8 = (s32[128,32]{1,0:T(8,128)}, s32[128,32]{1,0:T(8,128)S(1)}, u32[]{:S(2)}) copy-start(s32[128,32]{1,0:T(8,128)S(1)} %get-tuple-element.715) | copy-start | bytes 49156 | tf_op jit(solution)/shard_map/while
  1303.0 60.3 %all-to-all-start.2 = ((bf16[32,2,128]{2,1,0:T(2,128)(2,1)}), bf16[32,2,128]{2,1,0:T(2,128)(2,1)S(1)}, u32[]{:S(2)}, u32[]{:S(2)}) async-start(bf16[32,2,128]{2,1,0:T(2,128)(2,1)} %reshape.997), calls=%async_computation.2 | async-start | bytes 32768 | tf_op jit(solution)/shard_map/while/body/eval_jaxpr/all_to_all | solution.py:225
  1363.3 366.1 %all-to-all-start.3 = ((bf16[32,256,1024]{2,1,0:T(8,128)(2,1)}), bf16[32,256,1024]{2,1,0:T(8,128)(2,1)}, u32[]{:S(2)}, u32[]{:S(2)}) async-start(bf16[32,256,1024]{2,1,0:T(8,128)(2,1)} %bitcast.362), calls=%async_computation.3 | async-start | bytes 33554432 | tf_op jit(solution)/shard_map/while/body/eval_jaxpr/all_to_all | solution.py:224
  1754.9 93.5 %all-to-all-start.4 = ((f32[32,1,256]{2,1,0:T(1,128)}), f32[32,1,256]{2,1,0:T(1,128)}, u32[]{:S(2)}, u32[]{:S(2)}) async-start(f32[32,1,256]{2,1,0:T(1,128)} %all_to_all.59), calls=%async_computation.4 | async-start | bytes 65536 | tf_op jit(solution)/shard_map/while/body/eval_jaxpr/all_to_all | solution.py:233
  1886.3 117.8 %copy-start.15 = (f32[256,256]{1,0:T(8,128)}, f32[256,256]{1,0:T(8,128)S(1)}, u32[]{:S(2)}) copy-start(f32[256,256]{1,0:T(8,128)S(1)} %get-tuple-element.819) | copy-start | bytes 786436 | tf_op jit(solution)/shard_map/while
  1886.3 117.8 %copy-start.17 = (f32[256,256]{1,0:T(8,128)}, f32[256,256]{1,0:T(8,128)S(1)}, u32[]{:S(2)}) copy-start(f32[256,256]{1,0:T(8,128)S(1)} %get-tuple-element.818) | copy-start | bytes 786436 | tf_op jit(solution)/shard_map/while
  1888.2 115.8 %copy-start.8 = (s32[128,32]{1,0:T(8,128)}, s32[128,32]{1,0:T(8,128)S(1)}, u32[]{:S(2)}) copy-start(s32[128,32]{1,0:T(8,128)S(1)} %get-tuple-element.715) | copy-start | bytes 49156 | tf_op jit(solution)/shard_map/while
  1888.6 115.5 %copy-start.10 = (s32[128,32]{1,0:T(8,128)}, s32[128,32]{1,0:T(8,128)S(1)}, u32[]{:S(2)}) copy-start(s32[128,32]{1,0:T(8,128)S(1)} %add_select_fusion.24) | copy-start | bytes 49156 | tf_op jit(solution)/shard_map/while
  1940.9 63.2 %all-to-all-start.2 = ((bf16[32,2,128]{2,1,0:T(2,128)(2,1)}), bf16[32,2,128]{2,1,0:T(2,128)(2,1)S(1)}, u32[]{:S(2)}, u32[]{:S(2)}) async-start(bf16[32,2,128]{2,1,0:T(2,128)(2,1)} %reshape.997), calls=%async_computation.2 | async-start | bytes 32768 | tf_op jit(solution)/shard_map/while/body/eval_jaxpr/all_to_all | solution.py:225
  2004.1 366.1 %all-to-all-start.3 = ((bf16[32,256,1024]{2,1,0:T(8,128)(2,1)}), bf16[32,256,1024]{2,1,0:T(8,128)(2,1)}, u32[]{:S(2)}, u32[]{:S(2)}) async-start(bf16[32,256,1024]{2,1,0:T(8,128)(2,1)} %bitcast.362), calls=%async_computation.3 | async-start | bytes 33554432 | tf_op jit(solution)/shard_map/while/body/eval_jaxpr/all_to_all | solution.py:224
  2395.7 93.5 %all-to-all-start.4 = ((f32[32,1,256]{2,1,0:T(1,128)}), f32[32,1,256]{2,1,0:T(1,128)}, u32[]{:S(2)}, u32[]{:S(2)}) async-start(f32[32,1,256]{2,1,0:T(1,128)} %all_to_all.59), calls=%async_computation.4 | async-start | bytes 65536 | tf_op jit(solution)/shard_map/while/body/eval_jaxpr/all_to_all | solution.py:233
  2560.5 148.2 %all-reduce.14.cloned.1.call-start = ((), (), s32[]{:S(2)}) async-start(), calls=%async_computation.10 | async-start | bytes 2097152 | tf_op jit(solution)/shard_map/psum | solution.py:193
  2658.4 116.9 %all-reduce.12.cloned.1.call-start = ((), (), s32[]{:S(2)}) async-start(), calls=%async_computation.9 | async-start | bytes 4587520 | tf_op jit(solution)/shard_map/psum | solution.py:355
  (107 other events, 2532.0 us)
Sparse Core Ops, SparseCore 0:
  19.5 54.8 all-reduce.7
  1166.7 37.7 reduce-scatter.1
  2560.6 50.0 all-reduce.9
  2658.5 50.1 all-reduce.13
  2712.7 62.5 all-reduce.11
where the time goes:
time: 2800 us; the launch traced here: 2790 us
  waiting for transfers between devices  1540 us (55%)
  local copies, waits for them, and re-layouts  642 us (23%)
  other arithmetic  321 us (11%)
  blocking collectives  110 us (4%)
  matrix products  65.2 us (2%)
  starting transfers between devices  60.3 us (2%)
  loops' own time  33.8 us (1%)
    all_to_all x2, waiting for transfers between devices, gather_rows(): lax.all_to_all(fetched, ('dp', 'mp'), split_axis=0, concat_axis=0, tiled=...  702 us
    all_to_all x2, waiting for transfers between devices, scatter_back(): lax.all_to_all(send_grads, ('dp', 'mp'), split_axis=0, concat_axis=0, til...  628 us
    while x144, local copies, waits for them, and re-layouts  211 us
    gather x2, local copies, waits for them, and re-layouts, gather_rows(): picked = returned[owner_id, slot_rank].reshape(MEM_BLK, pick_count, width)  163 us
    scatter-add x2, other arithmetic, scatter_back(): table_acc.at[safe_rows.reshape(-1)].add(contrib.reshape(-1, width))  155 us
    gather x2, local copies, waits for them, and re-layouts, gather_rows(): fetched = value_table[jnp.maximum(arrived, 0)]  86.8 us
    gather x2, local copies, waits for them, and re-layouts, scatter_back(): value_table[safe_rows]  86.8 us
    gather x2, local copies, waits for them, and re-layouts, scatter_back(): weight_grad = answered[owner_id, slot_rank].reshape(MEM_BLK, pick_count)  65.5 us
  transfers between devices with their start and end apart: 13, of which 9 were waited for; matrix products, arithmetic and copies ran while one was open for 15% of the time, Pallas kernels for 0%

commit v1 on v0

--- a/solution.py
+++ b/solution.py
@@ -1,10 +1,13 @@
+import functools
 import jax
 import jax.numpy as jnp
 from jax import lax
+from jax.experimental import pallas as pl
+from jax.experimental.pallas import tpu as pltpu
 from jax.sharding import PartitionSpec as P
 
 HEAD_DIM = 64
-MEM_BLK = 128
+LANES = 128
 
 
 EPSILON = 1e-05
@@ -36,23 +39,123 @@
     return sigma * (1.0 + gate * (1.0 - sigma))
 
 
-def pick_scores(pick_blk, first_blk, second_blk, sub_count):
+NT = (((1,), (1,)), ((), ()))
+TN = (((0,), (0,)), ((), ()))
+
+
+def split_rows(ids, base, rows):
+    local = ids - base
+    here = (local >= 0) & (local < rows)
+    return jnp.where(here, local & (LANES - 1), 0), jnp.where(here, local >> 7, -1)
+
+
+def spread_kernel(unroll, base_ref, ids_ref, w_ref, out_ref, lo_s, hi_s, w_s, tiles):
+    brain = jnp.bfloat16
+    tokens, rows = out_ref.shape
+    high = rows // LANES
+    pad = max(high, 16)
+    lo, hi = split_rows(ids_ref[...], base_ref[0], rows)
+    lo_s[...] = lo.astype(jnp.float32)
+    hi_s[...] = hi.astype(jnp.float32)
+    w_s[...] = w_ref[...].astype(jnp.float32)
+    picks = ids_ref.shape[1]
+    low_at = lax.broadcasted_iota(jnp.int32, (LANES, picks), 0).astype(jnp.float32).astype(brain)
+    high_at = lax.broadcasted_iota(jnp.int32, (pad, picks), 0).astype(jnp.float32)
+    empty = jnp.zeros((pad, picks), brain)
+
+    def hot(t):
+        lo = jnp.broadcast_to(lo_s[pl.ds(t, 1), :], (LANES, picks)).astype(brain)
+        hi = jnp.broadcast_to(hi_s[pl.ds(t, 1), :], (pad, picks))
+        w = jnp.broadcast_to(w_s[pl.ds(t, 1), :], (pad, picks))
+        low_hot = jnp.where(lo == low_at, brain(1), brain(0))
+        high_hot = jnp.where(hi == high_at, w, 0.0).astype(brain)
+        return high_hot, low_hot
+
+    def step(i, carry):
+        for u in range(0, unroll, 2):
+            t = i * unroll + u
+            high_0, low_0 = hot(t)
+            high_1, low_1 = hot(t + 1)
+            left = jnp.concatenate(
+                [
+                    jnp.concatenate([high_0, empty], axis=1),
+                    jnp.concatenate([empty, high_1], axis=1),
+                ],
+                axis=0,
+            )
+            right = jnp.concatenate([low_0, low_1], axis=1)
+            tiles[pl.ds(t * pad, 2 * pad), :] = lax.dot_general(
+                left, right, NT, preferred_element_type=jnp.float32
+            )
+        return carry
+
+    lax.fori_loop(0, tokens // unroll, step, 0)
+    for a in range(high):
+        out_ref[:, a * LANES : (a + 1) * LANES] = tiles[pl.ds(a, tokens, stride=pad), :].astype(
+            brain
+        )
+
+
+def spread(ids, weights, base, rows, block=128, unroll=32):
+    tokens, picks = ids.shape
+    pad = max(rows // LANES, 16)
+    return pl.pallas_call(
+        functools.partial(spread_kernel, unroll),
+        grid=(tokens // block,),
+        in_specs=[
+            pl.BlockSpec(memory_space=pltpu.SMEM),
+            pl.BlockSpec((block, picks), lambda i: (i, 0)),
+            pl.BlockSpec((block, picks), lambda i: (i, 0)),
+        ],
+        out_specs=pl.BlockSpec((block, rows), lambda i: (i, 0)),
+        out_shape=jax.ShapeDtypeStruct((tokens, rows), jnp.bfloat16),
+        scratch_shapes=[pltpu.VMEM((block, picks), jnp.float32)] * 3
+        + [pltpu.VMEM((block * pad, LANES), jnp.float32)],
+        name="spread",
+    )(base, ids, weights)
+
+
+def answer_kernel(base_ref, grad_ref, table_ref, ids_ref, out_ref, all_s):
+    rows = table_ref.shape[0]
+    all_s[...] = lax.dot_general(
+        grad_ref[...], table_ref[...], NT, preferred_element_type=jnp.float32
+    )
+    lo, hi = split_rows(ids_ref[...], base_ref[0], rows)
+    total = jnp.zeros(ids_ref.shape, jnp.float32)
+    for a in range(rows // LANES):
+        found = jnp.take_along_axis(
+            all_s[:, a * LANES : (a + 1) * LANES], lo, axis=1, mode="promise_in_bounds"
+        )
+        total = jnp.where(hi == a, found, total)
+    out_ref[...] = total.astype(out_ref.dtype)
+
+
+def answer(ids, grads, table, base, block=256):
+    tokens, picks = ids.shape
+    rows, width = table.shape
+    return pl.pallas_call(
+        answer_kernel,
+        grid=(tokens // block,),
+        in_specs=[
+            pl.BlockSpec(memory_space=pltpu.SMEM),
+            pl.BlockSpec((block, width), lambda i: (i, 0)),
+            pl.BlockSpec((rows, width), lambda i: (0, 0)),
+            pl.BlockSpec((block, picks), lambda i: (i, 0)),
+        ],
+        out_specs=pl.BlockSpec((block, picks), lambda i: (i, 0)),
+        out_shape=jax.ShapeDtypeStruct((tokens, picks), jnp.float32),
+        scratch_shapes=[pltpu.VMEM((block, rows), jnp.float32)],
+        name="answer",
+    )(base, grads, table, ids)
+
+
+def pick_scores(picks, first, second, sub_count):
     columns = jnp.arange(sub_count, dtype=jnp.int32)
-    hit_first = (pick_blk // sub_count)[:, :, None] == columns
-    hit_second = (pick_blk % sub_count)[:, :, None] == columns
-    scores = jnp.sum(jnp.where(hit_first, first_blk[:, None, :], 0.0), axis=2)
-    scores = scores + jnp.sum(jnp.where(hit_second, second_blk[:, None, :], 0.0), axis=2)
+    hit_first = (picks // sub_count)[:, :, None] == columns
+    hit_second = (picks % sub_count)[:, :, None] == columns
+    scores = jnp.sum(jnp.where(hit_first, first[:, None, :], 0.0), axis=2)
+    scores = scores + jnp.sum(jnp.where(hit_second, second[:, None, :], 0.0), axis=2)
     return (jax.nn.softmax(scores, axis=-1), hit_first, hit_second)
-
-
-def slot_places(pick_blk, rows_here, owners):
-    flat = pick_blk.reshape(-1)
-    owner_id = flat // rows_here
-    local_row = flat % rows_here
-    owner_hits = (owner_id[:, None] == jnp.arange(owners, dtype=jnp.int32)).astype(jnp.int32)
-    before = jnp.cumsum(owner_hits, axis=0) - owner_hits
-    slot_rank = jnp.sum(before * owner_hits, axis=1)
-    return (owner_id, local_row, slot_rank)
 
 
 def per_device(
@@ -73,15 +176,11 @@
 ):
     floating = jnp.float32
     brain = jnp.bfloat16
-    length, width = block_in.shape
+    length = block_in.shape[0]
     col_width = col_weights.shape[2]
     heads_here = col_width // HEAD_DIM
-    owners = lax.axis_size("dp") * lax.axis_size("mp")
     rows_here = value_table.shape[0]
     pick_tok = pick_ids[:, 0, :]
-    pick_count = pick_tok.shape[1]
-    num_blocks = length // MEM_BLK
-    capacity = 2 * MEM_BLK * pick_count // owners
     query_rows = min(512, length)
     query_blocks = length // query_rows
     sub_count = mem_keys.shape[2]
@@ -157,35 +256,32 @@
     first_sub = matmul_nt(mem_query[:, :half_width], first_keys)
     second_sub = matmul_nt(mem_query[:, half_width:], second_keys)
 
-    def block_inputs(index):
-        start = index * MEM_BLK
-        pick_blk = lax.dynamic_slice_in_dim(pick_tok, start, MEM_BLK, 0)
-        first_blk = lax.dynamic_slice_in_dim(first_sub, start, MEM_BLK, 0)
-        second_blk = lax.dynamic_slice_in_dim(second_sub, start, MEM_BLK, 0)
-        return (pick_blk, first_blk, second_blk)
-
-    def gather_rows(index):
-        pick_blk, first_blk, second_blk = block_inputs(index)
-        weights_blk, hit_first, hit_second = pick_scores(pick_blk, first_blk, second_blk, sub_count)
-        owner_id, local_row, slot_rank = slot_places(pick_blk, rows_here, owners)
-        requests = (
-            jnp.full((owners, capacity), -1, jnp.int32).at[owner_id, slot_rank].set(local_row)
-        )
-        arrived = lax.all_to_all(requests, ("dp", "mp"), split_axis=0, concat_axis=0, tiled=True)
-        fetched = value_table[jnp.maximum(arrived, 0)]
-        returned = lax.all_to_all(fetched, ("dp", "mp"), split_axis=0, concat_axis=0, tiled=True)
-        picked = returned[owner_id, slot_rank].reshape(MEM_BLK, pick_count, width)
-        memory = jnp.einsum(
-            "tp,tpd->td", weights_blk.astype(brain), picked, preferred_element_type=floating
-        )
-        kept_rows = jnp.zeros((1, 1, 1), brain)
-        return (memory, arrived, kept_rows)
-
-    memory, arrivals, kept_all = lax.map(gather_rows, jnp.arange(num_blocks))
-    mem_cols = lax.psum_scatter(
-        memory.reshape(length, width), "mp", scatter_dimension=1, tiled=True
+    everyone = ("dp", "mp")
+    base = (
+        (lax.axis_index("dp") * lax.axis_size("mp") + lax.axis_index("mp")) * rows_here
+    ).reshape(1)
+    ids_all = lax.all_gather(
+        lax.all_gather(pick_tok, "mp", axis=1, tiled=True), "dp", axis=0, tiled=True
+    )
+    weights, hit_first, hit_second = pick_scores(pick_tok, first_sub, second_sub, sub_count)
+    weights_all = lax.all_gather(
+        lax.all_gather(weights.astype(brain), "mp", axis=1, tiled=True), "dp", axis=0, tiled=True
     )
     gate_act = jax.nn.silu(gate_pre)
+    low_branch_grad = (ADAPT_SCALE * matmul_nt(cotangent, up_row[1])).astype(brain)
+    gated_grad = matmul_nt(cotangent, row_weights[1]) + matmul(low_branch_grad, down_row[1])
+    mem_grad_cols = (gated_grad * gate_act).astype(brain)
+    mem_grad = lax.all_gather(
+        lax.all_gather(mem_grad_cols, "mp", axis=1, tiled=True), "dp", axis=0, tiled=True
+    )
+    spread_w = spread(ids_all, weights_all, base, rows_here)
+    partial = matmul(spread_w, value_table).astype(brain)
+    mem_cols = lax.psum_scatter(partial, "dp", scatter_dimension=0, tiled=True)
+    mem_cols = lax.psum_scatter(mem_cols, "mp", scatter_dimension=1, tiled=True).astype(floating)
+    answers = answer(ids_all, mem_grad, value_table, base)
+    weight_grad = lax.psum_scatter(answers, "dp", scatter_dimension=0, tiled=True)
+    weight_grad = lax.psum_scatter(weight_grad, "mp", scatter_dimension=1, tiled=True)
+    table_grad = matmul_tn(spread_w, mem_grad)
     gated = (mem_cols * gate_act).astype(brain)
     branch_part = matmul(gated, row_weights[1])
     low_branch_part = matmul_nt(gated, down_row[1])
@@ -196,60 +292,17 @@
     low_branch = low_branch_sum.astype(brain)
     block_out = (resid + branch_sum + ADAPT_SCALE * matmul(low_branch, up_row[1])).astype(brain)
     out_grad = cotangent.astype(floating)
-    low_branch_grad = (ADAPT_SCALE * matmul_nt(cotangent, up_row[1])).astype(brain)
     grad_up_branch = ADAPT_SCALE * matmul_tn(low_branch, cotangent)
-    gated_grad = matmul_nt(cotangent, row_weights[1]) + matmul(low_branch_grad, down_row[1])
     grad_down_branch = matmul_tn(low_branch_grad, gated)
-    mem_grad_cols = (gated_grad * gate_act).astype(brain)
     gate_grad = (gated_grad * mem_cols * silu_slope(gate_pre)).astype(brain)
-    mem_grad = lax.all_gather(mem_grad_cols, "mp", axis=1, tiled=True)
-
-    def scatter_back(table_acc, index):
-        pick_blk, first_blk, second_blk = block_inputs(index)
-        grad_blk = lax.dynamic_slice_in_dim(mem_grad, index * MEM_BLK, MEM_BLK, 0)
-        weights_blk, hit_first, hit_second = pick_scores(pick_blk, first_blk, second_blk, sub_count)
-        owner_id, local_row, slot_rank = slot_places(pick_blk, rows_here, owners)
-        token_of = jnp.arange(MEM_BLK * pick_count, dtype=jnp.int32) // pick_count
-        send_grads = (
-            jnp.zeros((owners, capacity, width), brain)
-            .at[owner_id, slot_rank]
-            .set(grad_blk[token_of])
-        )
-        send_weights = (
-            jnp.zeros((owners, capacity), brain)
-            .at[owner_id, slot_rank]
-            .set(weights_blk.astype(brain).reshape(-1))
-        )
-        got_grads, got_weights = (
-            lax.all_to_all(send_grads, ("dp", "mp"), split_axis=0, concat_axis=0, tiled=True),
-            lax.all_to_all(send_weights, ("dp", "mp"), split_axis=0, concat_axis=0, tiled=True),
-        )
-        safe_rows = jnp.maximum(arrivals[index], 0)
-        contrib = got_grads.astype(floating) * got_weights.astype(floating)[:, :, None]
-        table_acc = table_acc.at[safe_rows.reshape(-1)].add(contrib.reshape(-1, width))
-        products = jnp.einsum(
-            "scd,scd->sc", value_table[safe_rows], got_grads, preferred_element_type=floating
-        )
-        answered = lax.all_to_all(products, ("dp", "mp"), split_axis=0, concat_axis=0, tiled=True)
-        weight_grad = answered[owner_id, slot_rank].reshape(MEM_BLK, pick_count)
-        score_grad = weights_blk * (
-            weight_grad - jnp.sum(weights_blk * weight_grad, axis=-1, keepdims=True)
-        )
-        first_grad = jnp.sum(jnp.where(hit_first, score_grad[:, :, None], 0.0), axis=1).astype(
-            brain
-        )
-        second_grad = jnp.sum(jnp.where(hit_second, score_grad[:, :, None], 0.0), axis=1).astype(
-            brain
-        )
-        query_grad = jnp.concatenate(
-            [matmul(first_grad, first_keys), matmul(second_grad, second_keys)], axis=1
-        ).astype(brain)
-        return (table_acc, query_grad)
-
-    table_grad, query_grads = lax.scan(
-        scatter_back, jnp.zeros((rows_here, width), floating), jnp.arange(num_blocks)
-    )
-    query_grad = query_grads.reshape(length, col_width)
+    score_grad = weights * (
+        weight_grad - jnp.sum(weights * weight_grad, axis=-1, keepdims=True)
+    )
+    first_grad = jnp.sum(jnp.where(hit_first, score_grad[:, :, None], 0.0), axis=1).astype(brain)
+    second_grad = jnp.sum(jnp.where(hit_second, score_grad[:, :, None], 0.0), axis=1).astype(brain)
+    query_grad = jnp.concatenate(
+        [matmul(first_grad, first_keys), matmul(second_grad, second_keys)], axis=1
+    ).astype(brain)
     normed_two_part = matmul_nt(query_grad, col_weights[3]) + matmul_nt(gate_grad, col_weights[4])
     low_mem_part = ADAPT_SCALE * jnp.stack(
         [matmul_nt(query_grad, up_col[3]), matmul_nt(gate_grad, up_col[4])]

time: 2800 us -> 615 us (0.22)
  waiting for transfers between devices: 1540 us -> 280 us
  local copies, waits for them, and re-layouts: 642 us -> 16.9 us
  other arithmetic: 321 us -> 37.4 us
  starting transfers between devices: 60.3 us -> 0.82 us
  Pallas kernels: 0 us -> 53.5 us
  loops' own time: 33.8 us -> 0 us
  matrix products: 65.2 us -> 93.5 us
    all_to_all x8 -> x0, waiting for transfers between devices: 1330 us -> none  [the longest x2 702 us: gather_rows(): lax.all_to_all(fetched, ('dp', 'mp'), split_axis=0, concat_axis=0, tiled=...]
    gather x8 -> x0, local copies, waits for them, and re-layouts: 402 us -> none  [the longest x2 163 us: gather_rows(): picked = returned[owner_id, slot_rank].reshape(MEM_BLK, pick_count, width)]
    while x144 -> x0, local copies, waits for them, and re-layouts: 211 us -> none
    scatter-add x2 -> x0, other arithmetic: 155 us -> none  [scatter_back(): table_acc.at[safe_rows.reshape(-1)].add(contrib.reshape(-1, width))]
    reduce_scatter x1 -> x3, waiting for transfers between devices: 29.3 us -> 98.2 us  [the longest x1 49.7 us: per_device(): mem_cols = lax.psum_scatter(partial, 'dp', scatter_dimension=0, tiled=True)]
    all_to_all x8 -> x0, starting transfers between devices: 60.1 us -> none  [the longest x2 31.5 us: scatter_back(): lax.all_to_all(products, ('dp', 'mp'), split_axis=0, concat_axis=0, tiled...]
    pallas_call x0 -> x2, Pallas kernels: none -> 53.5 us  [the longest x1 37.9 us: spread(): pl.pallas_call(functools.partial(spread_kernel, unroll), grid=(tokens //...]
    dot_general x2 -> x0, other arithmetic: 49.8 us -> none  [scatter_back(): jnp.einsum('scd,scd->sc', value_table[safe_rows], got_grads, preferred_el...]
  transfers between devices with their start and end apart: 13 -> 10, of which waited for: 9 -> 9; matrix products, arithmetic and copies ran while one was open for 15% -> 11% of each run, Pallas kernels for 0% -> 0%
where the time goes in v1:
time: 615 us; the launch traced here: 612 us
  waiting for transfers between devices  280 us (46%)
  blocking collectives  114 us (19%)
  matrix products  93.5 us (15%)
  Pallas kernels  53.5 us (9%)
  other arithmetic  37.4 us (6%)
  between operations  17.1 us (3%)
  local copies, waits for them, and re-layouts  16.9 us (3%)
    psum x1, waiting for transfers between devices, per_device(): lax.psum(down_cols_all.astype(jnp.bfloat16), 'dp').astype(jnp.float32)  61.7 us
    reduce_scatter x1, waiting for transfers between devices, per_device(): mem_cols = lax.psum_scatter(partial, 'dp', scatter_dimension=0, tiled=True)  49.7 us
    pallas_call x1, Pallas kernels, spread(): pl.pallas_call(functools.partial(spread_kernel, unroll), grid=(tokens //...  37.9 us
    all_gather x1, waiting for transfers between devices, per_device(): lax.all_gather(lax.all_gather(mem_grad_cols, 'mp', axis=1, tiled=True), '...  34.6 us
    reduce_scatter x1, waiting for transfers between devices, per_device(): lax.psum_scatter(answers, 'dp', scatter_dimension=0, tiled=True)  34.1 us
    dot_general x13, matrix products, matmul(): return jnp.dot(left, right, preferred_element_type=jnp.float32)  32 us
    psum x1, waiting for transfers between devices, per_device(): lax.psum(branch_part.astype(jnp.bfloat16), 'mp').astype(jnp.float32)  28.9 us
    psum x1, waiting for transfers between devices, per_device(): lax.psum((normed_two_part, low_mem_part), 'mp')  23.5 us
  transfers between devices with their start and end apart: 10, of which 9 were waited for; matrix products, arithmetic and copies ran while one was open for 11% of the time, Pallas kernels for 0%

profile of v1, /device:TPU:0, one launch (start us, length us, event | category | flops | bytes accessed | tf_op | source)
XLA Modules:
  0.0 612.4 jit_solution(5104853827470323099)
XLA Ops:
  11.3 3.3 fusion.19
  21.5 15.7 %all-gather = s32[256,1,128]{0,1,2:T(1,128)S(1)} all-gather(s32[256,1,32]{0,1,2:T(1,128)S(1)} %copy.58), channel_id=2, replica_groups=mesh['dp'=8,'mp'=4] {'mp'}, dimensions={2}, use_global_device_ids=true | all-gather | bytes 163840 | tf_op jit(solution)/shard_map/all_gather | solution.py:264
  39.7 19.6 %psum.85 = bf16[256,16]{0,1:T(8,128)(2,1)S(1)} all-reduce(f32[256,16]{0,1:T(8,128)S(1)} %fusion.103), channel_id=1, replica_groups=mesh['dp'=8,'mp'=4] {'mp'}, use_global_device_ids=true, to_apply=%region_4.5 | all-reduce | flops 4096 | bytes 24576 | tf_op jit(solution)/shard_map/psum | solution.py:244
  60.2 16.6 %all-reduce.8.cloned.1.call-done = f32[256,1024]{1,0:T(8,128)} async-done(((f32[256,1024]{1,0:T(8,128)}), f32[256,1024]{1,0:T(8,128)}) %all-reduce.8.cloned.1.call-update) | async-done | bytes 1048592 | tf_op jit(solution)/shard_map/psum | solution.py:244
  84.2 5.1 select_reduce_fusion.2
  92.9 14.1 %all_gather.20 = bf16[256,128]{0,1:T(8,128)(2,1)} all-gather(bf16[256,32]{0,1:T(8,128)(2,1)} %copy.62), channel_id=1, replica_groups=mesh['dp'=8,'mp'=4] {'mp'}, dimensions={1}, use_global_device_ids=true | all-gather | bytes 81920 | tf_op jit(solution)/shard_map/all_gather | solution.py:268
  108.6 11.7 %all_gather.21.w_ref = bf16[2048,128]{1,0:T(8,128)(2,1)} all-gather(bf16[256,128]{1,0:T(8,128)(2,1)} %copy.63), channel_id=1, replica_groups=mesh['dp'=8,'mp'=4] {'dp'}, dimensions={0}, use_global_device_ids=true | all-gather | bytes 589824 | tf_op jit(solution)/shard_map/all_gather | solution.py:267
  120.3 37.9 %spread.1 = bf16[2048,2048]{1,0:T(8,128)(2,1)} custom-call(s32[1]{0:T(128)} %bitcast.16.base_ref, s32[2048,128]{1,0:T(8,128)} %bitcast.238, bf16[2048,128]{1,0:T(8,128)(2,1)} %all_gather.21.w_ref), custom_call_target="tpu_custom_call" | custom-call | tf_op jit(solution)/shard_map/spread/pallas_call | solution.py:102
  158.2 13.8 %convolution_convert_fusion = bf16[2048,1024]{1,0:T(8,128)(2,1)} fusion(bf16[2048,2048]{1,0:T(8,128)(2,1)} %spread.1, bf16[2048,1024]{1,0:T(8,128)(2,1)} %table_ref.1), kind=kOutput, calls=%fused_computation.6 | convolution fusion | flops 8592031744 | bytes 16777216 | tf_op jit(solution)/shard_map/dot_general | solution.py:18
  172.1 49.7 %reduce-scatter.7.cloned.1.call-done = bf16[256,1024]{1,0:T(8,128)(2,1)} async-done(((bf16[2048,1024]{1,0:T(8,128)(2,1)}), bf16[256,1024]{1,0:T(8,128)(2,1)}) %reduce-scatter.7.cloned.1.call-update) | async-done | bytes 524304 | tf_op jit(solution)/shard_map/reduce_scatter | solution.py:279
  229.1 14.4 %reduce-scatter.9.cloned.1.call-done = bf16[256,256]{1,0:T(8,128)(2,1)} async-done(((bf16[256,1024]{1,0:T(8,128)(2,1)}), bf16[256,256]{1,0:T(8,128)(2,1)}) %reduce-scatter.9.cloned.1.call-update) | async-done | bytes 131088 | tf_op jit(solution)/shard_map/reduce_scatter | solution.py:280
  245.6 16.6 %all_gather.22 = bf16[256,1024]{1,0:T(8,128)(2,1)} all-gather(bf16[256,256]{1,0:T(8,128)(2,1)S(1)} %get-tuple-element.77), channel_id=1, replica_groups=mesh['dp'=8,'mp'=4] {'mp'}, dimensions={1}, use_global_device_ids=true | all-gather | bytes 655360 | tf_op jit(solution)/shard_map/all_gather | solution.py:275
  262.5 34.6 %all-gather.5.cloned.1.call-done.grad_ref = bf16[2048,1024]{1,0:T(8,128)(2,1)} async-done(((bf16[256,1024]{1,0:T(8,128)(2,1)}), bf16[2048,1024]{1,0:T(8,128)(2,1)}) %all-gather.5.cloned.1.call-update) | async-done | bytes 4194320 | tf_op jit(solution)/shard_map/all_gather | solution.py:274
  297.1 15.6 %answer.1 = f32[2048,128]{1,0:T(8,128)} custom-call(s32[1]{0:T(128)} %bitcast.16.base_ref, bf16[2048,1024]{1,0:T(8,128)(2,1)} %all-gather.5.cloned.1.call-done.grad_ref, bf16[2048,1024]{1,0:T(8,128)(2,1)} %table_ref.1, s32[2048,128]{1,0:T(8,128)} %bitcast.239), custom_call_target="tpu_custom_call" | custom-call | tf_op jit(solution)/shard_map/answer/pallas_call | solution.py:136
  314.6 34.1 %reduce-scatter.11.cloned.1.call-done = f32[256,128]{1,0:T(8,128)} async-done(((f32[2048,128]{1,0:T(8,128)}), f32[256,128]{1,0:T(8,128)}) %reduce-scatter.11.cloned.1.call-update) | async-done | bytes 131088 | tf_op jit(solution)/shard_map/reduce_scatter | solution.py:282
  353.8 15.9 %reduce-scatter.13.cloned.1.call-done = f32[32,256]{1,0:T(8,128)} async-done(((f32[128,256]{1,0:T(8,128)}), f32[32,256]{1,0:T(8,128)}) %reduce-scatter.13.cloned.1.call-update) | async-done | bytes 32784
  373.5 5.8 select_reduce_fusion.1
  391.8 17.6 %psum.89 = bf16[2,256,16]{1,2,0:T(8,128)(2,1)S(1)} all-reduce(f32[2,256,16]{1,2,0:T(8,128)S(1)} %maximum_multiply_fusion), channel_id=1, replica_groups=mesh['dp'=8,'mp'=4] {'mp'}, use_global_device_ids=true, to_apply=%region_20.21 | all-reduce | flops 8192 | bytes 49152 | tf_op jit(solution)/shard_map/psum | solution.py:313
  413.7 23.5 %all-reduce.10.cloned.1.call-done = f32[256,1024]{1,0:T(8,128)} async-done(((f32[256,1024]{1,0:T(8,128)}), f32[256,1024]{1,0:T(8,128)}) %all-reduce.10.cloned.1.call-update) | async-done | bytes 1048592 | tf_op jit(solution)/shard_map/psum | solution.py:313
  459.0 18.2 %all-reduce.1 = (bf16[256,16]{0,1:T(8,128)(2,1)S(1)}, bf16[3,256,16]{1,2,0:T(8,128)(2,1)S(1)}) all-reduce(bf16[256,16]{0,1:T(8,128)(2,1)} %convolution_convert_fusion.8, bf16[3,256,16]{1,2,0:T(8,128)(2,1)} %fusion.31), channel_id=1, replica_groups=mesh['dp'=8,'mp'=4] {'mp'}, use_global_device_ids=true, to_apply=%region_13.14 | all-reduce | flops 16384 | bytes 65536 | tf_op jit(solution)/shard_map/psum | solution.py:290
  487.4 14.7 %fusion.136 = f32[2048,1024]{1,0:T(8,128)} fusion(bf16[2048,2048]{1,0:T(8,128)(2,1)} %spread.1, bf16[2048,1024]{1,0:T(8,128)(2,1)} %all-gather.5.cloned.1.call-done.grad_ref), kind=kOutput, calls=%fused_computation.226 | convolution fusion | flops 8589934592 | bytes 20971520 | tf_op jit(solution)/shard_map/dot_general | solution.py:28
  502.1 28.9 %all-reduce.14.cloned.1.call-done = (bf16[256,1024]{1,0:T(8,128)(2,1)}, bf16[256,1024]{1,0:T(8,128)(2,1)}) async-done(((bf16[256,1024]{1,0:T(8,128)(2,1)}, bf16[256,1024]{1,0:T(8,128)(2,1)}), (bf16[256,1024]{1,0:T(8,128)(2,1)}, bf16[256,1024]{1,0:T(8,128)(2,1)})) %all-reduce.14.cloned.1.call-update) | async-done | bytes 1048592 | tf_op jit(solution)/shard_map/psum | solution.py:289
  536.2 61.7 %all-reduce.12.cloned.1.call-done = (bf16[5,8,16,1024]{3,2,1,0:T(8,128)(2,1)}, bf16[5,8,16,256]{3,2,1,0:T(8,128)(2,1)}, bf16[2,8,16,256]{3,2,1,0:T(8,128)(2,1)}, bf16[2,8,16,1024]{3,2,1,0:T(8,128)(2,1)}) async-done(((bf16[5,8,16,1024]{3,2,1,0:T(8,128)(2,1)}, bf16[5,8,16,256]{3,2,1,0:T(8,128)(2,1)}, bf16[2,8,16,256]{3,2,1,0:T(8,128)(2,1)}, bf16[2,8,16,1024]{3,2,1,0:T(8,128)(2,1)}), ...) | async-done | bytes 2293776 | tf_op jit(solution)/shard_map/psum | solution.py:408
  597.9 3.2 convert_element_type.249
  (202 shorter events, 103.0 us)
Async XLA Ops:
  8.0 68.7 %all-reduce.8.cloned.1.call-start = ((), (), s32[]{:S(2)}) async-start(), calls=%async_computation.4 | async-start | bytes 2097152 | tf_op jit(solution)/shard_map/psum | solution.py:244
  8.9 70.3 %copy-start.28 = (f32[1,1024]{1,0:T(1,128)}, f32[1,1024]{1,0:T(1,128)S(1)}, u32[]{:S(2)}) copy-start(f32[1,1024]{1,0:T(1,128)S(1)} %get-tuple-element.84) | copy-start | bytes 12292
  19.0 19.9 %copy-start.34 = (f32[4,256]{1,0:T(4,128)}, f32[4,256]{1,0:T(4,128)S(1)}, u32[]{:S(2)}) copy-start(f32[4,256]{1,0:T(4,128)S(1)} %fusion.41) | copy-start | bytes 12292
  19.4 39.9 %copy-start.12 = (bf16[4,64,256]{2,1,0:T(8,128)(2,1)}, bf16[4,64,256]{2,1,0:T(8,128)(2,1)S(1)}, u32[]{:S(2)}) copy-start(bf16[4,64,256]{2,1,0:T(8,128)(2,1)S(1)} %convolution_convert_fusion.3) | copy-start | bytes 393220
  20.7 99.6 %all-gather.7.cloned.1.call-start = ((), (), s32[]{:S(2)}) async-start(), calls=%async_computation.10 | async-start | bytes 1179648 | tf_op jit(solution)/shard_map/all_gather | solution.py:263
  38.0 183.7 %reduce-scatter.7.cloned.1.call-start = ((), (), s32[]{:S(2)}) async-start(), calls=%async_computation.5 | async-start | bytes 4718592 | tf_op jit(solution)/shard_map/reduce_scatter | solution.py:279
  59.3 20.1 %copy-start.24 = (bf16[256,16]{0,1:T(8,128)(2,1)}, bf16[256,16]{0,1:T(8,128)(2,1)S(1)}, u32[]{:S(2)}) copy-start(bf16[256,16]{0,1:T(8,128)(2,1)S(1)} %psum.85) | copy-start | bytes 24580
  59.4 29.9 %copy-start.10 = (s32[256,32]{1,0:T(8,128)}, s32[256,32]{1,0:T(8,128)S(1)}, u32[]{:S(2)}) copy-start(s32[256,32]{1,0:T(8,128)S(1)} %copy.61) | copy-start | bytes 98308
  172.0 71.5 %reduce-scatter.9.cloned.1.call-start = ((), (), s32[]{:S(2)}) async-start(), calls=%async_computation.6 | async-start | bytes 655360 | tf_op jit(solution)/shard_map/reduce_scatter | solution.py:280
  221.7 75.3 %all-gather.5.cloned.1.call-start = ((), (), s32[]{:S(2)}) async-start(), calls=%async_computation.7 | async-start | bytes 4718592 | tf_op jit(solution)/shard_map/all_gather | solution.py:274
  262.2 86.6 %reduce-scatter.11.cloned.1.call-start = ((), (), s32[]{:S(2)}) async-start(), calls=%async_computation.8 | async-start | bytes 1179648 | tf_op jit(solution)/shard_map/reduce_scatter | solution.py:282
  312.7 57.1 %reduce-scatter.13.cloned.1.call-start = ((), (), s32[]{:S(2)}) async-start(), calls=%async_computation.11 | async-start | bytes 163840
  350.5 86.7 %all-reduce.10.cloned.1.call-start = ((), (), s32[]{:S(2)}) async-start(), calls=%async_computation.9 | async-start | bytes 2097152 | tf_op jit(solution)/shard_map/psum | solution.py:313
  373.5 13.6 %copy-start.9 = (bf16[256,256]{1,0:T(8,128)(2,1)S(1)}, bf16[256,256]{1,0:T(8,128)(2,1)}, u32[]{:S(2)}) copy-start(bf16[256,256]{1,0:T(8,128)(2,1)} %get-tuple-element.78) | copy-start | bytes 393220
  386.0 144.9 %all-reduce.14.cloned.1.call-start = ((), (), s32[]{:S(2)}) async-start(), calls=%async_computation.13 | async-start | bytes 2097152 | tf_op jit(solution)/shard_map/psum | solution.py:289
  390.8 48.2 %copy-start.38 = (f32[256]{0:T(256)S(1)}, f32[256]{0:T(256)}, u32[]{:S(2)}) copy-start(f32[256]{0:T(256)} %copy-done.37) | copy-start | bytes 3076
  390.8 48.2 %copy-start.44 = (f32[256]{0:T(256)S(1)}, f32[256]{0:T(256)}, u32[]{:S(2)}) copy-start(f32[256]{0:T(256)} %get-tuple-element.88) | copy-start | bytes 3076
  444.5 14.4 %copy-start.25 = (bf16[256,16]{0,1:T(8,128)(2,1)S(1)}, bf16[256,16]{0,1:T(8,128)(2,1)}, u32[]{:S(2)}) copy-start(bf16[256,16]{0,1:T(8,128)(2,1)} %copy-done.24) | copy-start | bytes 24580
  458.9 24.6 %copy-start.39 = (f32[8]{0:T(128)S(1)}, f32[8]{0:T(128)}, u32[]{:S(2)}) copy-start(f32[8]{0:T(128)} %compare_convert_fusion) | copy-start | bytes 100
  480.6 117.3 %all-reduce.12.cloned.1.call-start = ((), (), s32[]{:S(2)}) async-start(), calls=%async_computation.12 | async-start | bytes 4587520 | tf_op jit(solution)/shard_map/psum | solution.py:408
  487.4 43.6 %copy-start.31 = (bf16[3,256,16]{1,2,0:T(8,128)(2,1)S(1)}, bf16[3,256,16]{1,2,0:T(8,128)(2,1)}, u32[]{:S(2)}) copy-start(bf16[3,256,16]{1,2,0:T(8,128)(2,1)} %copy-done.30) | copy-start | bytes 73732
  487.4 43.5 %copy-start.36 = (f32[1,1024]{1,0:T(1,128)S(1)}, f32[1,1024]{1,0:T(1,128)}, u32[]{:S(2)}) copy-start(f32[1,1024]{1,0:T(1,128)} %copy-done.35) | copy-start | bytes 12292
  502.1 32.8 %copy-start.41 = (f32[256]{0:T(256)S(1)}, f32[256]{0:T(256)}, u32[]{:S(2)}) copy-start(f32[256]{0:T(256)} %get-tuple-element.86) | copy-start | bytes 3076
  502.1 32.8 %copy-start.43 = (f32[256]{0:T(256)S(1)}, f32[256]{0:T(256)}, u32[]{:S(2)}) copy-start(f32[256]{0:T(256)} %copy-done.42) | copy-start | bytes 3076
  (31 other events, 132.3 us)
Sparse Core Ops, SparseCore 0:
  20.8 55.8 all-reduce.7
  221.9 21.5 reduce-scatter.8
  350.6 19.1 reduce-scatter.12
  386.1 51.0 all-reduce.9
  480.7 50.1 all-reduce.13
  535.4 62.4 all-reduce.11
Sparse Core Ops, SparseCore 1:
  38.1 24.4 all-gather.6
  172.1 49.6 reduce-scatter.6
  262.3 34.7 all-gather.4
  312.8 35.9 reduce-scatter.10

commit v2 on v1

--- a/solution.py
+++ b/solution.py
@@ -147,6 +147,448 @@
         scratch_shapes=[pltpu.VMEM((block, rows), jnp.float32)],
         name="answer",
     )(base, grads, table, ids)
+
+
+MESH = pl.DeviceIdType.MESH
+
+
+def partner(index, bit):
+    return index + bit - 2 * bit * ((index // bit) % 2)
+
+
+def remote(src, dst, sems, slot, device):
+    return pltpu.make_async_remote_copy(
+        src_ref=src,
+        dst_ref=dst,
+        send_sem=sems.at[0, slot],
+        recv_sem=sems.at[1, slot],
+        device_id=device,
+        device_id_type=MESH,
+    )
+
+
+def greet(devices):
+    barrier = pltpu.get_barrier_semaphore()
+    for device in devices:
+        pl.semaphore_signal(barrier, inc=1, device_id=device, device_id_type=MESH)
+    pl.semaphore_wait(barrier, len(devices))
+
+
+def hot_rows(lo_s, hi_s, w_s, tiles, tokens, pad):
+    brain = jnp.bfloat16
+    picks = lo_s.shape[1]
+    low_at = lax.broadcasted_iota(jnp.int32, (LANES, picks), 0).astype(jnp.float32).astype(brain)
+    high_at = lax.broadcasted_iota(jnp.int32, (pad, picks), 0).astype(jnp.float32)
+    empty = jnp.zeros((pad, picks), brain)
+
+    def hot(t):
+        lo = jnp.broadcast_to(lo_s[t : t + 1, :], (LANES, picks)).astype(brain)
+        hi = jnp.broadcast_to(hi_s[t : t + 1, :], (pad, picks))
+        w = jnp.broadcast_to(w_s[t : t + 1, :], (pad, picks))
+        low_hot = jnp.where(lo == low_at, brain(1), brain(0))
+        high_hot = jnp.where(hi == high_at, w, 0.0).astype(brain)
+        return high_hot, low_hot
+
+    for t in range(0, tokens, 2):
+        high_0, low_0 = hot(t)
+        high_1, low_1 = hot(t + 1)
+        left = jnp.concatenate(
+            [
+                jnp.concatenate([high_0, empty], axis=1),
+                jnp.concatenate([empty, high_1], axis=1),
+            ],
+            axis=0,
+        )
+        right = jnp.concatenate([low_0, low_1], axis=1)
+        tiles[t * pad : (t + 2) * pad, :] = lax.dot_general(
+            left, right, NT, preferred_element_type=jnp.float32
+        )
+
+
+def memory_kernel(
+    seqs,
+    parts,
+    table_hbm,
+    ids_hbm,
+    weights_ref,
+    grads_ref,
+    memory_ref,
+    answers_ref,
+    table_grad_hbm,
+    table_v,
+    ids_v,
+    w_all,
+    g_all,
+    spread_v,
+    tiles,
+    lo_s,
+    hi_s,
+    w_s,
+    part_own,
+    part_sib,
+    got_core,
+    got_x,
+    got_y,
+    got_z,
+    ans_own,
+    ans_sib,
+    ans_core,
+    ans_plane,
+    ans_z,
+    all_s,
+    tg_v,
+    local_sems,
+    sems_w,
+    sems_g,
+    sems_m,
+    sems_a,
+):
+    floating, brain = jnp.float32, jnp.bfloat16
+    d = lax.axis_index("dp")
+    m = lax.axis_index("mp")
+    rows, width = table_v.shape
+    picks_here, length = weights_ref.shape
+    picks = picks_here * parts
+    cols = width // parts
+    half = length // 2
+    core = partner(d, 1)
+    x_side = partner(d, 2)
+    y_side = partner(d, 4)
+    corner = partner(x_side, 4)
+    mine, chip_x, chip_y, chip_d = d // 2, x_side // 2, y_side // 2, corner // 2
+    z_of = [lax.rem(m + k, parts) for k in range(parts)]
+    table_in = pltpu.make_async_copy(table_hbm, table_v, local_sems.at[0])
+    ids_in = pltpu.make_async_copy(ids_hbm, ids_v, local_sems.at[1])
+    ids_in.start()
+    table_in.start()
+    at = lambda place: {"dp": place, "mp": m}
+    deep = lambda k: {"dp": d, "mp": z_of[k]}
+    greet(
+        [deep(k) for k in range(1, parts)]
+        + [at(x_side), at(y_side), at(corner), at(core)]
+    )
+    pick_rows = pl.ds(pl.multiple_of(m * picks_here, 16), picks_here)
+    my_cols = pl.ds(pl.multiple_of(m * cols, LANES), cols)
+    seq_rows = lambda s: pl.ds(pl.multiple_of(s * length, 16), length)
+    w_all[d, pick_rows, :] = weights_ref[...]
+    g_all[seq_rows(d), my_cols] = grads_ref[...]
+    w_z = [
+        remote(weights_ref, w_all.at[d, pick_rows, :], sems_w, k, deep(k)) for k in range(1, parts)
+    ]
+    g_z = [
+        remote(grads_ref, g_all.at[seq_rows(d), my_cols], sems_g, k, deep(k))
+        for k in range(1, parts)
+    ]
+    for c in w_z:
+        c.start()
+    for c in g_z:
+        c.start()
+    for c in w_z:
+        c.wait_recv()
+    w_plane = [
+        remote(w_all.at[d], w_all.at[d], sems_w, 4 + i, at(p))
+        for i, p in enumerate((x_side, y_side, corner, core))
+    ]
+    for c in w_plane:
+        c.start()
+    for c in w_plane[:3]:
+        c.wait_recv()
+    w_core = [
+        remote(w_all.at[p], w_all.at[p], sems_w, 8 + i, at(core))
+        for i, p in enumerate((x_side, y_side, corner))
+    ]
+    for c in w_core:
+        c.start()
+    w_plane[3].wait_recv()
+    for c in w_core:
+        c.wait_recv()
+    ids_in.wait()
+
+    block = lo_s.shape[0]
+    base = (d * parts + m) * rows
+    pad = tiles.shape[0] // block
+
+    def build(i, carry):
+        here = pl.ds(pl.multiple_of(i * block, block), block)
+        lo, hi = split_rows(ids_v[here, :], base, rows)
+        lo_s[...] = lo.astype(floating)
+        hi_s[...] = hi.astype(floating)
+        per_seq = length // block
+        w_t = w_all[i // per_seq, :, pl.ds(pl.multiple_of((i % per_seq) * block, block), block)]
+        w_s[...] = jnp.transpose(w_t.astype(floating))
+        hot_rows(lo_s, hi_s, w_s, tiles, block, pad)
+        for a in range(rows // LANES):
+            spread_v[here, a * LANES : (a + 1) * LANES] = tiles[
+                pl.ds(a, block, stride=pad), :
+            ].astype(brain)
+        return carry
+
+    blocks = seqs * length // block
+    cuts = [0, blocks // 8, (9 * blocks) // 16, (13 * blocks) // 16, blocks]
+    lax.fori_loop(cuts[0], cuts[1], build, 0)
+    for c in g_z:
+        c.wait_recv()
+    whole = lambda s: g_all.at[seq_rows(s)]
+    part = lambda s, h: g_all.at[pl.ds(pl.multiple_of(s * length + h * half, 16), half)]
+    g_one = [
+        remote(whole(d), whole(d), sems_g, 4 + i, at(p)) for i, p in enumerate((x_side, y_side, core))
+    ]
+    for c in g_one:
+        c.start()
+    lax.fori_loop(cuts[1], cuts[2], build, 0)
+    g_one[0].wait_recv()
+    g_one[1].wait_recv()
+    g_two = [
+        remote(part(y_side, 0), part(y_side, 0), sems_g, 7, at(x_side)),
+        remote(part(x_side, 1), part(x_side, 1), sems_g, 8, at(y_side)),
+        remote(whole(x_side), whole(x_side), sems_g, 9, at(core)),
+        remote(whole(y_side), whole(y_side), sems_g, 10, at(core)),
+    ]
+    for c in g_two:
+        c.start()
+    lax.fori_loop(cuts[2], cuts[3], build, 0)
+    g_two[0].wait_recv()
+    g_two[1].wait_recv()
+    g_three = remote(whole(corner), whole(corner), sems_g, 11, at(core))
+    g_three.start()
+    lax.fori_loop(cuts[3], cuts[4], build, 0)
+
+    table_in.wait()
+    sib_core = core % 2
+
+    def partial_of(seq):
+        return jnp.dot(
+            spread_v[seq_rows(seq), :], table_v[...], preferred_element_type=floating
+        ).astype(brain)
+
+    to_core = [
+        remote(part_sib.at[c], got_core.at[c], sems_m, c, at(core)) for c in range(seqs // 2)
+    ]
+    for c in range(seqs // 2):
+        part_sib[c] = partial_of(2 * c + sib_core)
+        to_core[c].start()
+
+    def own_part(c, carry):
+        part_own[c] = partial_of(2 * c + d % 2)
+        return carry
+
+    lax.fori_loop(0, seqs // 2, own_part, 0)
+    for c in to_core:
+        c.wait_recv()
+
+    def fold(c, carry):
+        part_own[c] = (part_own[c].astype(floating) + got_core[c].astype(floating)).astype(brain)
+        return carry
+
+    lax.fori_loop(0, seqs // 2, fold, 0)
+    upper, lower = pl.ds(0, half), pl.ds(half, half)
+    m_one = [
+        remote(part_own.at[chip_d, upper], got_x.at[0], sems_m, 4, at(x_side)),
+        remote(part_own.at[chip_d, lower], got_y.at[0], sems_m, 5, at(y_side)),
+        remote(part_own.at[chip_x, upper], got_x.at[1], sems_m, 6, at(x_side)),
+        remote(part_own.at[chip_y, lower], got_y.at[1], sems_m, 7, at(y_side)),
+    ]
+    for c in m_one:
+        c.start()
+
+    for c in g_two[2:]:
+        c.wait_recv()
+    g_one[2].wait_recv()
+    g_three.wait_recv()
+
+    def answers_of(seq):
+        all_s[...] = lax.dot_general(
+            g_all[seq_rows(seq), :], table_v[...], NT, preferred_element_type=floating
+        )
+        lo, hi = split_rows(ids_v[seq_rows(seq), :], base, rows)
+        total = jnp.zeros((length, picks), floating)
+        for a in range(rows // LANES):
+            found = jnp.take_along_axis(
+                all_s[:, a * LANES : (a + 1) * LANES], lo, axis=1, mode="promise_in_bounds"
+            )
+            total = jnp.where(hi == a, found, total)
+        return jnp.transpose(total).astype(brain)
+
+    def sib_answers(c, carry):
+        ans_sib[c] = answers_of(2 * c + sib_core)
+        return carry
+
+    def own_answers(c, carry):
+        ans_own[c] = answers_of(2 * c + d % 2)
+        return carry
+
+    lax.fori_loop(0, seqs // 2, sib_answers, 0)
+    a_core = remote(ans_sib, ans_core, sems_a, 0, at(core))
+    a_core.start()
+    m_one[0].wait_recv()
+    m_one[1].wait_recv()
+    part_own[chip_y, upper] = (
+        part_own[chip_y, upper].astype(floating) + got_x[0].astype(floating)
+    ).astype(brain)
+    part_own[chip_x, lower] = (
+        part_own[chip_x, lower].astype(floating) + got_y[0].astype(floating)
+    ).astype(brain)
+    m_two = [
+        remote(part_own.at[chip_x, lower], got_x.at[2], sems_m, 8, at(x_side)),
+        remote(part_own.at[chip_y, upper], got_y.at[2], sems_m, 9, at(y_side)),
+    ]
+    for c in m_two:
+        c.start()
+    lax.fori_loop(0, seqs // 2, own_answers, 0)
+    a_core.wait_recv()
+    ans_own[...] = (ans_own[...].astype(floating) + ans_core[...].astype(floating)).astype(brain)
+    a_plane = [
+        remote(ans_own.at[chip], ans_plane.at[i], sems_a, 1 + i, at(p))
+        for i, (chip, p) in enumerate(((chip_x, x_side), (chip_y, y_side), (chip_d, corner)))
+    ]
+    for c in m_one[2:]:
+        c.wait_recv()
+    for c in m_two:
+        c.wait_recv()
+    part_own[mine, upper] = (
+        part_own[mine, upper].astype(floating)
+        + got_x[1].astype(floating)
+        + got_y[2].astype(floating)
+    ).astype(brain)
+    part_own[mine, lower] = (
+        part_own[mine, lower].astype(floating)
+        + got_x[2].astype(floating)
+        + got_y[1].astype(floating)
+    ).astype(brain)
+    cols_of = lambda k: pl.ds(pl.multiple_of(z_of[k] * cols, LANES), cols)
+    m_z = [
+        remote(part_own.at[mine, :, cols_of(k)], got_z.at[k - 1], sems_m, 9 + k, deep(k))
+        for k in range(1, parts)
+    ]
+    for c in a_plane:
+        c.start()
+    for c in m_z:
+        c.start()
+
+    tg_block = tg_v.shape[1]
+
+    def tg_out(i):
+        return pltpu.make_async_copy(
+            tg_v.at[i % 2],
+            table_grad_hbm.at[pl.ds(pl.multiple_of(i * tg_block, tg_block), tg_block)],
+            local_sems.at[2 + i % 2],
+        )
+
+    def tg_step(i):
+        tg_v[i % 2] = lax.dot_general(
+            spread_v[:, i * tg_block : (i + 1) * tg_block],
+            g_all[...],
+            TN,
+            preferred_element_type=floating,
+        )
+
+    steps = rows // tg_block
+    for i in range(steps):
+        if i >= 2:
+            tg_out(i - 2).wait()
+        tg_step(i)
+        tg_out(i).start()
+        if i == steps // 4:
+            for c in a_plane:
+                c.wait_recv()
+            ans_own[mine] = (
+                ans_own[mine].astype(floating)
+                + ans_plane[0].astype(floating)
+                + ans_plane[1].astype(floating)
+                + ans_plane[2].astype(floating)
+            ).astype(brain)
+            a_z = [
+                remote(
+                    ans_own.at[mine, pl.ds(pl.multiple_of(z_of[k] * picks_here, 16), picks_here)],
+                    ans_z.at[k - 1],
+                    sems_a,
+                    3 + k,
+                    deep(k),
+                )
+                for k in range(1, parts)
+            ]
+            for c in a_z:
+                c.start()
+    for c in a_z:
+        c.wait_recv()
+    answers_ref[...] = (
+        ans_own[mine, pick_rows, :].astype(floating)
+        + ans_z[0].astype(floating)
+        + ans_z[1].astype(floating)
+        + ans_z[2].astype(floating)
+    )
+    for c in m_z:
+        c.wait_recv()
+    memory_ref[...] = (
+        part_own[mine, :, my_cols].astype(floating)
+        + got_z[0].astype(floating)
+        + got_z[1].astype(floating)
+        + got_z[2].astype(floating)
+    )
+    for i in range(max(steps - 2, 0), steps):
+        tg_out(i).wait()
+    for c in w_z + g_z + w_plane + w_core + g_one + g_two + [g_three]:
+        c.wait_send()
+    for c in to_core + m_one + m_two + [a_core] + a_plane + m_z + a_z:
+        c.wait_send()
+
+
+def memory_call(seqs, parts, table, ids, weights_t, grads):
+    rows, width = table.shape
+    picks_here, length = weights_t.shape
+    tokens, picks = ids.shape
+    cols = width // parts
+    block, tg_block = 128, 256
+    pad = max(rows // LANES, 16)
+    floating, brain = jnp.float32, jnp.bfloat16
+    vmem = pl.BlockSpec(memory_space=pltpu.VMEM)
+    anywhere = pl.BlockSpec(memory_space=pl.ANY)
+    scratch = [
+        ((rows, width), brain),
+        ((tokens, picks), jnp.int32),
+        ((seqs, picks, length), brain),
+        ((tokens, width), brain),
+        ((tokens, rows), brain),
+        ((block * pad, LANES), floating),
+        ((block, picks), floating),
+        ((block, picks), floating),
+        ((block, picks), floating),
+        ((seqs // 2, length, width), brain),
+        ((seqs // 2, length, width), brain),
+        ((seqs // 2, length, width), brain),
+        ((3, length // 2, width), brain),
+        ((3, length // 2, width), brain),
+        ((parts - 1, length, cols), brain),
+        ((seqs // 2, picks, length), brain),
+        ((seqs // 2, picks, length), brain),
+        ((seqs // 2, picks, length), brain),
+        ((3, picks, length), brain),
+        ((parts - 1, picks_here, length), brain),
+        ((length, rows), floating),
+        ((2, tg_block, width), floating),
+    ]
+    return pl.pallas_call(
+        functools.partial(memory_kernel, seqs, parts),
+        in_specs=[anywhere, anywhere, vmem, vmem],
+        out_specs=[vmem, vmem, anywhere],
+        out_shape=[
+            jax.ShapeDtypeStruct((length, cols), floating),
+            jax.ShapeDtypeStruct((picks_here, length), floating),
+            jax.ShapeDtypeStruct((rows, width), floating),
+        ],
+        scratch_shapes=[pltpu.VMEM(shape, kind) for shape, kind in scratch]
+        + [
+            pltpu.SemaphoreType.DMA((4,)),
+            pltpu.SemaphoreType.DMA((2, 12)),
+            pltpu.SemaphoreType.DMA((2, 12)),
+            pltpu.SemaphoreType.DMA((2, 14)),
+            pltpu.SemaphoreType.DMA((2, 8)),
+        ],
+        compiler_params=pltpu.CompilerParams(
+            collective_id=0, has_side_effects=True, vmem_limit_bytes=58 * 2**20
+        ),
+        name="memory",
+    )(table, ids, weights_t, grads)
 
 
 def pick_scores(picks, first, second, sub_count):
@@ -264,24 +706,31 @@
         lax.all_gather(pick_tok, "mp", axis=1, tiled=True), "dp", axis=0, tiled=True
     )
     weights, hit_first, hit_second = pick_scores(pick_tok, first_sub, second_sub, sub_count)
-    weights_all = lax.all_gather(
-        lax.all_gather(weights.astype(brain), "mp", axis=1, tiled=True), "dp", axis=0, tiled=True
-    )
     gate_act = jax.nn.silu(gate_pre)
     low_branch_grad = (ADAPT_SCALE * matmul_nt(cotangent, up_row[1])).astype(brain)
     gated_grad = matmul_nt(cotangent, row_weights[1]) + matmul(low_branch_grad, down_row[1])
     mem_grad_cols = (gated_grad * gate_act).astype(brain)
-    mem_grad = lax.all_gather(
-        lax.all_gather(mem_grad_cols, "mp", axis=1, tiled=True), "dp", axis=0, tiled=True
-    )
-    spread_w = spread(ids_all, weights_all, base, rows_here)
-    partial = matmul(spread_w, value_table).astype(brain)
-    mem_cols = lax.psum_scatter(partial, "dp", scatter_dimension=0, tiled=True)
-    mem_cols = lax.psum_scatter(mem_cols, "mp", scatter_dimension=1, tiled=True).astype(floating)
-    answers = answer(ids_all, mem_grad, value_table, base)
-    weight_grad = lax.psum_scatter(answers, "dp", scatter_dimension=0, tiled=True)
-    weight_grad = lax.psum_scatter(weight_grad, "mp", scatter_dimension=1, tiled=True)
-    table_grad = matmul_tn(spread_w, mem_grad)
+    seqs, parts = lax.axis_size("dp"), lax.axis_size("mp")
+    if seqs == 8:
+        mem_cols, answers_t, table_grad = memory_call(
+            seqs, parts, value_table, ids_all, weights.astype(brain).T, mem_grad_cols
+        )
+        weight_grad = answers_t.T
+    else:
+        weights_all = lax.all_gather(
+            lax.all_gather(weights.astype(brain), "mp", axis=1, tiled=True), "dp", axis=0, tiled=True
+        )
+        mem_grad = lax.all_gather(
+            lax.all_gather(mem_grad_cols, "mp", axis=1, tiled=True), "dp", axis=0, tiled=True
+        )
+        spread_w = spread(ids_all, weights_all, base, rows_here)
+        partial = matmul(spread_w, value_table).astype(brain)
+        mem_cols = lax.psum_scatter(partial, "dp", scatter_dimension=0, tiled=True)
+        mem_cols = lax.psum_scatter(mem_cols, "mp", scatter_dimension=1, tiled=True).astype(floating)
+        answers = answer(ids_all, mem_grad, value_table, base)
+        weight_grad = lax.psum_scatter(answers, "dp", scatter_dimension=0, tiled=True)
+        weight_grad = lax.psum_scatter(weight_grad, "mp", scatter_dimension=1, tiled=True)
+        table_grad = matmul_tn(spread_w, mem_grad)
     gated = (mem_cols * gate_act).astype(brain)
     branch_part = matmul(gated, row_weights[1])
     low_branch_part = matmul_nt(gated, down_row[1])

time: 615 us -> 455 us (0.74)
  waiting for transfers between devices: 280 us -> 137 us
  blocking collectives: 114 us -> 76.2 us
  Pallas kernels: 53.5 us -> 89.1 us
  matrix products: 93.5 us -> 59.2 us
  other arithmetic: 37.4 us -> 53.3 us
    reduce_scatter x3 -> x0, waiting for transfers between devices: 98.2 us -> none  [the longest x1 49.7 us: per_device(): mem_cols = lax.psum_scatter(partial, 'dp', scatter_dimension=0, tiled=True)]
    all_gather x3 -> x0, blocking collectives: 42.5 us -> none  [the longest x1 16.6 us: per_device(): lax.all_gather(mem_grad_cols, 'mp', axis=1, tiled=True)]
    pallas_call x2 -> x1, Pallas kernels: 53.5 us -> 89.1 us  [memory_call(): pl.pallas_call(functools.partial(memory_kernel, seqs, parts), in_specs=[a...]
    all_gather x1 -> x0, waiting for transfers between devices: 34.6 us -> none  [per_device(): lax.all_gather(lax.all_gather(mem_grad_cols, 'mp', axis=1, tiled=True), '...]
    unnamed x11 -> x5, waiting for transfers between devices: 16.1 us -> 0.08 us
    dot_general x13 -> x12, matrix products: 32 us -> 17.3 us  [matmul(): return jnp.dot(left, right, preferred_element_type=jnp.float32)]
    dot_general x7 -> x6, matrix products: 21 us -> 6.71 us  [matmul_tn(): lax.dot_general(left, right, (((0,), (0,)), ((), ())), preferred_element_...]
    psum x1, waiting for transfers between devices: 28.9 us -> 40.4 us  [per_device(): lax.psum(branch_part.astype(jnp.bfloat16), 'mp').astype(jnp.float32)]
  transfers between devices with their start and end apart: 10 -> 5, of which waited for: 9 -> 4; matrix products, arithmetic and copies ran while one was open for 11% -> 15% of each run, Pallas kernels for 0% -> 0%
where the time goes in v2:
time: 455 us; the launch traced here: 452 us
  waiting for transfers between devices  137 us (30%)
  Pallas kernels  89.1 us (20%)
  blocking collectives  76.2 us (17%)
  matrix products  59.2 us (13%)
  other arithmetic  53.3 us (12%)
  local copies, waits for them, and re-layouts  20.9 us (5%)
  between operations  16.7 us (4%)
    pallas_call x1, Pallas kernels, memory_call(): pl.pallas_call(functools.partial(memory_kernel, seqs, parts), in_specs=[a...  89.1 us
    psum x1, waiting for transfers between devices, per_device(): lax.psum(down_cols_all.astype(jnp.bfloat16), 'dp').astype(jnp.float32)  61.8 us
    psum x1, waiting for transfers between devices, per_device(): lax.psum(branch_part.astype(jnp.bfloat16), 'mp').astype(jnp.float32)  40.4 us
    psum x1, blocking collectives, per_device(): lax.psum((normed_two_part, low_mem_part), 'mp')  22.3 us
    psum x1, waiting for transfers between devices, per_device(): lax.psum((normed_two_part, low_mem_part), 'mp')  20.9 us
    psum x1, blocking collectives, per_device(): att_sum, low_sum = lax.psum((att_part, low_part), 'mp')  19.3 us
    psum x1, blocking collectives, per_device(): lax.psum(low_branch_part.astype(jnp.bfloat16), 'mp').astype(jnp.float32)  18.9 us
    dot_general x12, matrix products, matmul(): return jnp.dot(left, right, preferred_element_type=jnp.float32)  17.3 us
  transfers between devices with their start and end apart: 5, of which 4 were waited for; matrix products, arithmetic and copies ran while one was open for 15% of the time, Pallas kernels for 0%

profile of v2, /device:TPU:0, one launch (start us, length us, event | category | flops | bytes accessed | tf_op | source)
XLA Modules:
  0.0 452.2 jit_solution(6148592666668729554)
XLA Ops:
  11.4 2.4 fusion.19
  18.5 15.7 %all-gather = s32[256,1,128]{0,1,2:T(1,128)S(1)} all-gather(s32[256,1,32]{0,1,2:T(1,128)S(1)} %copy.56), channel_id=2, replica_groups=mesh['dp'=8,'mp'=4] {'mp'}, dimensions={2}, use_global_device_ids=true | all-gather | bytes 163840 | tf_op jit(solution)/shard_map/all_gather | solution.py:706
  36.5 19.3 %psum.85 = bf16[256,16]{0,1:T(8,128)(2,1)S(1)} all-reduce(f32[256,16]{0,1:T(8,128)S(1)} %fusion.102), channel_id=1, replica_groups=mesh['dp'=8,'mp'=4] {'mp'}, use_global_device_ids=true, to_apply=%region_4.5 | all-reduce | flops 4096 | bytes 24576 | tf_op jit(solution)/shard_map/psum | solution.py:686
  55.8 2.1 fusion.49
  60.9 13.5 %all-reduce.8.cloned.1.call-done = f32[256,1024]{1,0:T(8,128)} async-done(((f32[256,1024]{1,0:T(8,128)}), f32[256,1024]{1,0:T(8,128)}) %all-reduce.8.cloned.1.call-update) | async-done | bytes 1048592 | tf_op jit(solution)/shard_map/psum | solution.py:686
  80.6 9.2 %select_reduce_fusion.3 = f32[256,32]{1,0:T(8,128)} fusion(f32[256,256]{1,0:T(8,128)S(1)} %fusion.79, s32[256,32]{1,0:T(8,128)S(1)} %copy.58), kind=kLoop, calls=%fused_computation.4 | loop fusion | flops 6283264 | bytes 327680 | tf_op jit(solution)/shard_map/reduce_sum | solution.py:598
  92.4 9.5 %select_reduce_fusion.2 = f32[256,32]{1,0:T(8,128)} fusion(f32[256,256]{1,0:T(8,128)S(1)} %fusion.77, s32[256,32]{1,0:T(8,128)} %copy.59), kind=kLoop, calls=%fused_computation.2 | loop fusion | flops 6283264 | bytes 327680 | tf_op jit(solution)/shard_map/reduce_sum | solution.py:599
  109.2 2.0 multiply_convert_fusion.8
  111.2 89.1 %memory.1 = (f32[256,256]{1,0:T(8,128)}, f32[32,256]{1,0:T(8,128)}, f32[2048,1024]{1,0:T(8,128)}) custom-call(bf16[2048,1024]{1,0:T(8,128)(2,1)} %table_hbm.1, s32[2048,128]{1,0:T(8,128)} %bitcast.249, bf16[32,256]{1,0:T(8,128)(2,1)} %convert_bitcast_fusion.weights_ref, bf16[256,256]{1,0:T(8,128)(2,1)} %get-tuple-element.99.grads_ref), custom_call_target="tpu_custom_call" | custom-call | tf_op jit(solution)/shard_map/memory/pallas_call | solution.py:570
  204.1 5.9 %select_reduce_fusion.1 = (bf16[256,256]{1,0:T(8,128)(2,1)S(1)}, bf16[256,256]{1,0:T(8,128)(2,1)S(1)}) fusion(f32[256,32]{1,0:T(8,128)} %copy.62, s32[256,32]{1,0:T(8,128)S(1)} %copy.58, s32[256,32]{1,0:T(8,128)} %copy.59), kind=kLoop, calls=%fused_computation.1 | loop fusion | flops 12451840 | bytes 360448 | tf_op jit(solution)/shard_map/reduce_sum | solution.py:750
  217.4 2.4 convolution_add_fusion
  221.2 22.3 %psum.89 = bf16[2,256,16]{1,2,0:T(8,128)(2,1)S(1)} all-reduce(f32[2,256,16]{1,2,0:T(8,128)} %maximum_multiply_fusion), channel_id=1, replica_groups=mesh['dp'=8,'mp'=4] {'mp'}, use_global_device_ids=true, to_apply=%region_16.17 | all-reduce | flops 8192 | bytes 49152 | tf_op jit(solution)/shard_map/psum | solution.py:762
  248.8 1.9 fusion.51
  250.7 2.1 convolution_convert_fusion
  252.9 20.9 %all-reduce.10.cloned.1.call-done = f32[256,1024]{1,0:T(8,128)} async-done(((f32[256,1024]{1,0:T(8,128)}), f32[256,1024]{1,0:T(8,128)}) %all-reduce.10.cloned.1.call-update) | async-done | bytes 1048592 | tf_op jit(solution)/shard_map/psum | solution.py:762
  283.9 3.1 fusion.14
  290.5 18.9 %all-reduce.1 = (bf16[256,16]{0,1:T(8,128)(2,1)}, bf16[3,256,16]{1,2,0:T(8,128)(2,1)}) all-reduce(bf16[256,16]{0,1:T(8,128)(2,1)} %convolution_convert_fusion.7, bf16[3,256,16]{1,2,0:T(8,128)(2,1)} %fusion.31), channel_id=1, replica_groups=mesh['dp'=8,'mp'=4] {'mp'}, use_global_device_ids=true, to_apply=%region_11.12 | all-reduce | flops 16384 | bytes 65536 | tf_op jit(solution)/shard_map/psum | solution.py:739
  309.4 2.0 fusion.95
  321.2 2.0 multiply_convert_fusion
  323.3 40.4 %all-reduce.14.cloned.1.call-done = (bf16[256,1024]{1,0:T(8,128)(2,1)}, bf16[256,1024]{1,0:T(8,128)(2,1)}) async-done(((bf16[256,1024]{1,0:T(8,128)(2,1)}, bf16[256,1024]{1,0:T(8,128)(2,1)}), (bf16[256,1024]{1,0:T(8,128)(2,1)}, bf16[256,1024]{1,0:T(8,128)(2,1)})) %all-reduce.14.cloned.1.call-update) | async-done | bytes 1048592 | tf_op jit(solution)/shard_map/psum | solution.py:738
  365.5 2.2 fusion.18
  368.9 61.8 %all-reduce.12.cloned.1.call-done = (bf16[5,8,16,1024]{3,2,1,0:T(8,128)(2,1)}, bf16[5,8,16,256]{3,2,1,0:T(8,128)(2,1)}, bf16[2,8,16,256]{3,2,1,0:T(8,128)(2,1)}, bf16[2,8,16,1024]{3,2,1,0:T(8,128)(2,1)}) async-done(((bf16[5,8,16,1024]{3,2,1,0:T(8,128)(2,1)}, bf16[5,8,16,256]{3,2,1,0:T(8,128)(2,1)}, bf16[2,8,16,256]{3,2,1,0:T(8,128)(2,1)}, bf16[2,8,16,1024]{3,2,1,0:T(8,128)(2,1)}), ...) | async-done | bytes 2293776 | tf_op jit(solution)/shard_map/psum | solution.py:857
  430.7 3.2 convert_element_type.239
  436.7 8.4 %copy.93 = f32[2048,1024]{1,0:T(8,128)} copy(f32[2048,1024]{1,0:T(8,128)} %get-tuple-element.116) | data formatting | bytes 16777216
  (211 shorter events, 75.3 us)
Async XLA Ops:
  8.0 66.4 %all-reduce.8.cloned.1.call-start = ((), (), s32[]{:S(2)}) async-start(), calls=%async_computation | async-start | bytes 2097152 | tf_op jit(solution)/shard_map/psum | solution.py:686
  8.9 6.3 %copy-start.52 = (f32[1,1024]{1,0:T(1,128)}, f32[1,1024]{1,0:T(1,128)S(1)}, u32[]{:S(2)}) copy-start(f32[1,1024]{1,0:T(1,128)S(1)} %get-tuple-element.90) | copy-start | bytes 12292
  8.9 67.9 %copy-start.44 = (f32[1,1024]{1,0:T(1,128)}, f32[1,1024]{1,0:T(1,128)S(1)}, u32[]{:S(2)}) copy-start(f32[1,1024]{1,0:T(1,128)S(1)} %get-tuple-element.89) | copy-start | bytes 12292
  16.4 42.3 %copy-start.12 = (bf16[4,64,256]{2,1,0:T(8,128)(2,1)}, bf16[4,64,256]{2,1,0:T(8,128)(2,1)S(1)}, u32[]{:S(2)}) copy-start(bf16[4,64,256]{2,1,0:T(8,128)(2,1)S(1)} %convolution_convert_fusion.2) | copy-start | bytes 393220
  16.4 39.4 %copy-start.4 = (bf16[256,1024]{1,0:T(8,128)(2,1)S(1)}, bf16[256,1024]{1,0:T(8,128)(2,1)}, u32[]{:S(2)}) copy-start(bf16[256,1024]{1,0:T(8,128)(2,1)} %param.15) | copy-start | bytes 1572868
  18.4 92.8 %all-gather.4.cloned.1.call-start = ((), (), s32[]{:S(2)}) async-start(), calls=%async_computation.2 | async-start | bytes 1179648 | tf_op jit(solution)/shard_map/all_gather | solution.py:705
  35.0 238.8 %all-reduce.10.cloned.1.call-start = ((), (), s32[]{:S(2)}) async-start(), calls=%async_computation.1 | async-start | bytes 2097152 | tf_op jit(solution)/shard_map/psum | solution.py:762
  55.8 21.2 %copy-start.39 = (bf16[256,16]{0,1:T(8,128)(2,1)}, bf16[256,16]{0,1:T(8,128)(2,1)S(1)}, u32[]{:S(2)}) copy-start(bf16[256,16]{0,1:T(8,128)(2,1)S(1)} %psum.85) | copy-start | bytes 24580
  78.8 137.9 %copy-start.38 = (bf16[2,256,16]{1,2,0:T(8,128)(2,1)}, bf16[2,256,16]{1,2,0:T(8,128)(2,1)S(1)}, u32[]{:S(2)}) copy-start(bf16[2,256,16]{1,2,0:T(8,128)(2,1)S(1)} %fusion.32) | copy-start | bytes 49156
  111.2 89.2 %copy-start.21 = (f32[256,32]{0,1:T(8,128)S(1)}, f32[256,32]{0,1:T(8,128)}, u32[]{:S(2)}) copy-start(f32[256,32]{0,1:T(8,128)} %copy-done.20) | copy-start | bytes 98308
  111.2 89.2 %copy-start.47 = (f32[256]{0:T(256)S(1)}, f32[256]{0:T(256)}, u32[]{:S(2)}) copy-start(f32[256]{0:T(256)} %copy-done.46) | copy-start | bytes 3076
  111.2 89.2 %copy-start.51 = (f32[256]{0:T(256)S(1)}, f32[256]{0:T(256)}, u32[]{:S(2)}) copy-start(f32[256]{0:T(256)} %copy-done.50) | copy-start | bytes 3076
  204.1 10.9 %copy-start.19 = (f32[256,256]{1,0:T(8,128)S(1)}, f32[256,256]{1,0:T(8,128)}, u32[]{:S(2)}) copy-start(f32[256,256]{1,0:T(8,128)} %copy-done.18) | copy-start | bytes 786436
  204.1 10.9 %copy-start.29 = (f32[256,256]{1,0:T(8,128)S(1)}, f32[256,256]{1,0:T(8,128)}, u32[]{:S(2)}) copy-start(f32[256,256]{1,0:T(8,128)} %get-tuple-element.100) | copy-start | bytes 786436
  204.1 10.9 %copy-start.30 = (f32[256,256]{1,0:T(8,128)S(1)}, f32[256,256]{1,0:T(8,128)}, u32[]{:S(2)}) copy-start(f32[256,256]{1,0:T(8,128)} %get-tuple-element.56) | copy-start | bytes 786436
  219.8 143.9 %all-reduce.14.cloned.1.call-start = ((), (), s32[]{:S(2)}) async-start(), calls=%async_computation.4 | async-start | bytes 2097152 | tf_op jit(solution)/shard_map/psum | solution.py:738
  289.6 23.8 %copy-start.25 = (f32[2,16,1024]{2,1,0:T(8,128)S(1)}, f32[2,16,1024]{2,1,0:T(8,128)}, u32[]{:S(2)}) copy-start(f32[2,16,1024]{2,1,0:T(8,128)} %fusion.51) | copy-start | bytes 393220
  290.5 25.6 %copy-start.42 = (f32[1,16,256]{2,1,0:T(8,128)S(1)}, f32[1,16,256]{2,1,0:T(8,128)}, u32[]{:S(2)}) copy-start(f32[1,16,256]{2,1,0:T(8,128)} %convolution_bitcast_fusion.4) | copy-start | bytes 49156
  313.3 117.4 %all-reduce.12.cloned.1.call-start = ((), (), s32[]{:S(2)}) async-start(), calls=%async_computation.3 | async-start | bytes 4587520 | tf_op jit(solution)/shard_map/psum | solution.py:857
  316.1 47.6 %copy-start.48 = (bf16[3,256,16]{1,2,0:T(8,128)(2,1)S(1)}, bf16[3,256,16]{1,2,0:T(8,128)(2,1)}, u32[]{:S(2)}) copy-start(bf16[3,256,16]{1,2,0:T(8,128)(2,1)} %get-tuple-element.77) | copy-start | bytes 73732
  316.1 47.6 %copy-start.53 = (f32[1,1024]{1,0:T(1,128)S(1)}, f32[1,1024]{1,0:T(1,128)}, u32[]{:S(2)}) copy-start(f32[1,1024]{1,0:T(1,128)} %copy-done.52) | copy-start | bytes 12292
  323.3 42.2 %copy-start.45 = (bf16[256,16]{0,1:T(8,128)(2,1)S(1)}, bf16[256,16]{0,1:T(8,128)(2,1)}, u32[]{:S(2)}) copy-start(bf16[256,16]{0,1:T(8,128)(2,1)} %get-tuple-element.76) | copy-start | bytes 24580
  323.3 44.4 %copy-start.56 = (f32[256]{0:T(256)S(1)}, f32[256]{0:T(256)}, u32[]{:S(2)}) copy-start(f32[256]{0:T(256)} %get-tuple-element.91) | copy-start | bytes 3076
  323.3 44.4 %copy-start.58 = (f32[256]{0:T(256)S(1)}, f32[256]{0:T(256)}, u32[]{:S(2)}) copy-start(f32[256]{0:T(256)} %copy-done.57) | copy-start | bytes 3076
  (40 other events, 103.0 us)
Sparse Core Ops, SparseCore 0:
  18.5 55.8 all-reduce.7
  219.9 53.7 all-reduce.9
  313.5 50.2 all-reduce.13
  368.2 62.4 all-reduce.11
Sparse Core Ops, SparseCore 1:
  35.0 24.4 all-gather.3

commit v3 on v1

--- a/solution.py
+++ b/solution.py
@@ -147,6 +147,839 @@
         scratch_shapes=[pltpu.VMEM((block, rows), jnp.float32)],
         name="answer",
     )(base, grads, table, ids)
+
+
+MESH = pl.DeviceIdType.MESH
+SIDE = 128
+
+
+class Refs:
+    pass
+
+
+def partner(index, bit):
+    return index + bit - 2 * bit * ((index // bit) % 2)
+
+
+def remote(src, dst, sems, slot, device):
+    return pltpu.make_async_remote_copy(
+        src_ref=src,
+        dst_ref=dst,
+        send_sem=sems.at[0, slot],
+        recv_sem=sems.at[1, slot],
+        device_id=device,
+        device_id_type=MESH,
+    )
+
+
+def greet(devices):
+    barrier = pltpu.get_barrier_semaphore()
+    for device in devices:
+        pl.semaphore_signal(barrier, inc=1, device_id=device, device_id_type=MESH)
+    pl.semaphore_wait(barrier, len(devices))
+
+
+def start(copies):
+    for c in copies:
+        c.start()
+
+
+def arrive(copies):
+    for c in copies:
+        c.wait_recv()
+
+
+def nt(left, right):
+    return lax.dot_general(left, right, NT, preferred_element_type=jnp.float32)
+
+
+def tn(left, right):
+    return lax.dot_general(left, right, TN, preferred_element_type=jnp.float32)
+
+
+def padded(values, rows=SIDE):
+    return jnp.concatenate(
+        [values, jnp.zeros((rows - values.shape[0], values.shape[1]), values.dtype)], axis=0
+    )
+
+
+def hot_rows(lo_s, hi_s, w_s, tiles, tokens, pad):
+    brain = jnp.bfloat16
+    picks = lo_s.shape[1]
+    low_at = lax.broadcasted_iota(jnp.int32, (LANES, picks), 0).astype(jnp.float32).astype(brain)
+    high_at = lax.broadcasted_iota(jnp.int32, (pad, picks), 0).astype(jnp.float32)
+    empty = jnp.zeros((pad, picks), brain)
+
+    def hot(t):
+        lo = jnp.broadcast_to(lo_s[t : t + 1, :], (LANES, picks)).astype(brain)
+        hi = jnp.broadcast_to(hi_s[t : t + 1, :], (pad, picks))
+        w = jnp.broadcast_to(w_s[t : t + 1, :], (pad, picks))
+        low_hot = jnp.where(lo == low_at, brain(1), brain(0))
+        high_hot = jnp.where(hi == high_at, w, 0.0).astype(brain)
+        return high_hot, low_hot
+
+    for t in range(0, tokens, 2):
+        high_0, low_0 = hot(t)
+        high_1, low_1 = hot(t + 1)
+        left = jnp.concatenate(
+            [
+                jnp.concatenate([high_0, empty], axis=1),
+                jnp.concatenate([empty, high_1], axis=1),
+            ],
+            axis=0,
+        )
+        right = jnp.concatenate([low_0, low_1], axis=1)
+        tiles[t * pad : (t + 2) * pad, :] = lax.dot_general(
+            left, right, NT, preferred_element_type=jnp.float32
+        )
+
+
+def block_kernel(names, seqs, parts, *refs):
+    n = Refs()
+    for name, ref in zip(names, refs):
+        setattr(n, name, ref)
+    floating, brain = jnp.float32, jnp.bfloat16
+    d = lax.axis_index("dp")
+    m = lax.axis_index("mp")
+    length, width = n.block_in.shape
+    cols = width // parts
+    quarter = length // parts
+    rows = n.table_v.shape[0]
+    picks_here = n.pick_ids.shape[1]
+    picks = picks_here * parts
+    half = length // 2
+    subs = n.mem_keys.shape[2]
+    half_width = n.mem_keys.shape[3]
+    heads = cols // HEAD_DIM
+
+    core, x_side, y_side = partner(d, 1), partner(d, 2), partner(d, 4)
+    corner = partner(x_side, 4)
+    mine, chip_x, chip_y, chip_d = d // 2, x_side // 2, y_side // 2, corner // 2
+    z_of = [lax.rem(m + k, parts) for k in range(parts)]
+    sent = []
+
+    def at(place):
+        return {"dp": place, "mp": m}
+
+    def deep(k):
+        return {"dp": d, "mp": z_of[k]}
+
+    def go(copies):
+        start(copies)
+        sent.extend(copies)
+        return copies
+
+    def z_scatter(send, got, sems):
+        return go([remote(send.at[z_of[k]], got.at[k - 1], sems, k, deep(k)) for k in range(1, parts)])
+
+    def z_gather(ref, sems, slot=0):
+        return go([remote(ref.at[m], ref.at[m], sems, slot + k, deep(k)) for k in range(1, parts)])
+
+    def near_gather(ref, sems):
+        places = (x_side, y_side, corner, core)
+        return go([remote(ref.at[d], ref.at[d], sems, 4 + i, at(p)) for i, p in enumerate(places)])
+
+    def core_gather(ref, sems):
+        places = (x_side, y_side, corner)
+        return go([remote(ref.at[p], ref.at[p], sems, 8 + i, at(core)) for i, p in enumerate(places)])
+
+    table_in = pltpu.make_async_copy(n.table, n.table_v, n.local_sems.at[0])
+    table_in.start()
+    adapter = n.adapter_ids[0]
+
+    n.pick_wide[...] = jnp.zeros(n.pick_wide.shape, jnp.int32)
+    n.pick_wide[:, :picks_here] = n.pick_ids[...]
+    pick_rows = pl.ds(pl.multiple_of(m * picks_here, 16), picks_here)
+    n.picks_own[...] = (
+        jnp.transpose(n.pick_wide[...].astype(floating))[:picks_here].astype(jnp.int32)
+        + adapter * 65536
+    )
+    greet(
+        [deep(k) for k in range(1, parts)] + [at(x_side), at(y_side), at(corner), at(core)]
+    )
+    i_z = go(
+        [
+            remote(n.picks_own, n.ids_t.at[d, pick_rows, :], n.sems_i, k, deep(k))
+            for k in range(1, parts)
+        ]
+    )
+    n.ids_t[d, pick_rows, :] = n.picks_own[...]
+
+    inputs = n.block_in[...].astype(floating)
+    gain_one, gain_two = n.norm_gains[0:1, :], n.norm_gains[1:2, :]
+    scale_one = lax.rsqrt(jnp.mean(inputs * inputs, axis=1, keepdims=True) + EPSILON)
+    normed_one = (inputs * scale_one * gain_one).astype(brain)
+    n.normed_one[...] = normed_one
+    rank = n.col_down.shape[2]
+    down_att = jnp.concatenate([n.col_down[j, adapter] for j in range(3)], axis=0)
+    down_mem = jnp.concatenate([n.col_down[j, adapter] for j in (3, 4)], axis=0)
+    n.up_att[...] = jnp.zeros(n.up_att.shape, brain)
+    n.up_mem[...] = jnp.zeros(n.up_mem.shape, brain)
+    for j in range(3):
+        n.up_att[j * rank : (j + 1) * rank, j * cols : (j + 1) * cols] = n.col_up[j, adapter]
+    for j in range(2):
+        n.up_mem[j * rank : (j + 1) * rank, j * cols : (j + 1) * cols] = n.col_up[3 + j, adapter]
+    low_att = nt(normed_one, down_att).astype(brain)
+    n.low_att[...] = low_att
+    for j in range(3):
+        n.proj[:, j * cols : (j + 1) * cols] = (
+            jnp.dot(normed_one, n.col_weights[j], preferred_element_type=floating)
+            + ADAPT_SCALE
+            * jnp.dot(low_att, n.up_att[:, j * cols : (j + 1) * cols], preferred_element_type=floating)
+        ).astype(brain)
+    arrive(i_z)
+    i_near = near_gather(n.ids_t, n.sems_i)
+
+    segment = jnp.broadcast_to(n.segment_ids[...].astype(floating), (length, length))
+    ahead = lax.broadcasted_iota(jnp.int32, (length, length), 1) <= lax.broadcasted_iota(
+        jnp.int32, (length, length), 0
+    )
+    allowed = (segment == jnp.transpose(segment)) & ahead
+    lane = lax.broadcasted_iota(jnp.int32, (length, LANES), 1)
+    sides = LANES // HEAD_DIM
+
+    def pair_of(which, pair):
+        first = which * cols + pair * LANES
+        return n.proj[:, first : first + LANES]
+
+    for pair in range(heads // sides):
+        query2, key2, value2 = (pair_of(w, pair) for w in range(3))
+        mixed = jnp.zeros((length, LANES), floating)
+        for side in range(sides):
+            own = lane // HEAD_DIM == side
+            logits = 0.125 * nt(jnp.where(own, query2, brain(0)), key2)
+            logits = jnp.where(allowed, logits, -1e30)
+            expos = jnp.exp(logits - jnp.max(logits, axis=1, keepdims=True))
+            probs = expos / jnp.sum(expos, axis=1, keepdims=True)
+            n.probs[pair * sides + side] = probs
+            out = jnp.dot(probs.astype(brain), value2, preferred_element_type=floating)
+            mixed = jnp.where(own, out, mixed)
+        n.att_out[:, pair * LANES : (pair + 1) * LANES] = mixed.astype(brain)
+    att_out = n.att_out[...]
+    row_down = [n.row_down[j, adapter] for j in range(2)]
+    row_up = [n.row_up[j, adapter] for j in range(2)]
+    down_att_out = padded(row_down[0])
+    low_part = nt(att_out, down_att_out)
+    att_part = jnp.dot(att_out, n.row_weights[0], preferred_element_type=floating)
+    att_part = att_part + ADAPT_SCALE * jnp.dot(
+        low_part.astype(brain), padded(row_up[0]), preferred_element_type=floating
+    )
+    n.sum_send[0, :, :, :width] = att_part.astype(brain).reshape(parts, quarter, width)
+    n.sum_send[0, :, :, width:] = low_part.astype(brain).reshape(parts, quarter, SIDE)
+    r_att = z_scatter(n.sum_send.at[0], n.sum_got.at[0], n.sems_z.at[0])
+    arrive(i_near[:3])
+    i_core = core_gather(n.ids_t, n.sems_i)
+
+    cotangent = n.cotangent[...]
+    low_branch_grad = (ADAPT_SCALE * nt(cotangent, padded(row_up[1]))).astype(brain)
+    n.low_branch_grad[...] = low_branch_grad
+    n.gated_grad[...] = nt(cotangent, n.row_weights[1]) + jnp.dot(
+        low_branch_grad, padded(row_down[1]), preferred_element_type=floating
+    )
+    arrive(i_near[3:])
+    arrive(i_core)
+    base = (d * parts + m) * rows
+
+    def turn(s, carry):
+        local = n.ids_t[s] % 65536 - base
+        here = (local >= 0) & (local < rows)
+        turned = jnp.transpose(jnp.where(here, local, -1).astype(floating)).astype(jnp.int32)
+        n.ids_v[pl.ds(pl.multiple_of(s * length, 16), length), :] = turned
+        n.who[s] = n.ids_t[s, 0:8, 0:LANES] // 65536
+        return carry
+
+    lax.fori_loop(0, seqs, turn, 0)
+
+    my_rows = pl.ds(pl.multiple_of(m * quarter, 16), quarter)
+
+    def total_of(i):
+        total = n.sum_send[i, m].astype(floating)
+        for k in range(parts - 1):
+            total = total + n.sum_got[i, k].astype(floating)
+        return total
+
+    arrive(r_att)
+    total = total_of(0)
+    resid = n.block_in[my_rows, :].astype(floating) + total[:, :width]
+    n.resid[...] = resid
+    scale_two = lax.rsqrt(jnp.mean(resid * resid, axis=1, keepdims=True) + EPSILON)
+    n.gath_two[m, :, :width] = (resid * scale_two * gain_two).astype(brain)
+    n.gath_two[m, :, width:] = total[:, width:].astype(brain)
+    arrive(z_gather(n.gath_two, n.sems_z.at[1]))
+
+    normed_two = n.gath_two[:, :, :width].reshape(length, width)
+    low_mem = nt(normed_two, down_mem).astype(brain)
+    n.low_mem[...] = low_mem
+    mem_query = (
+        jnp.dot(normed_two, n.col_weights[3], preferred_element_type=floating)
+        + ADAPT_SCALE * jnp.dot(low_mem, n.up_mem[:, :cols], preferred_element_type=floating)
+    ).astype(brain)
+    sub_one = nt(mem_query[:, :half_width], n.mem_keys[0, 0])
+    sub_two = nt(mem_query[:, half_width:], n.mem_keys[1, 0])
+    wide = n.pick_wide[...]
+
+    def chosen(table, index):
+        found = jnp.zeros(index.shape, floating)
+        for c in range(subs // LANES):
+            taken = jnp.take_along_axis(
+                table[:, c * LANES : (c + 1) * LANES],
+                index % LANES,
+                axis=1,
+                mode="promise_in_bounds",
+            )
+            found = jnp.where(index // LANES == c, taken, found)
+        return found
+
+    scores = chosen(sub_one, wide // subs) + chosen(sub_two, wide % subs)
+    scores = jnp.where(lane < picks_here, scores, -1e30)
+    expos = jnp.exp(scores - jnp.max(scores, axis=1, keepdims=True))
+    weights = expos / jnp.sum(expos, axis=1, keepdims=True)
+    n.weights_t[...] = jnp.transpose(weights)[:picks_here]
+    n.weights_own[...] = n.weights_t[...].astype(brain)
+    w_z = go(
+        [
+            remote(n.weights_own, n.w_all.at[d, pick_rows, :], n.sems_w, k, deep(k))
+            for k in range(1, parts)
+        ]
+    )
+    n.w_all[d, pick_rows, :] = n.weights_own[...]
+    gate_pre = jnp.dot(
+        normed_two, n.col_weights[4], preferred_element_type=floating
+    ) + ADAPT_SCALE * jnp.dot(low_mem, n.up_mem[:, cols:], preferred_element_type=floating)
+    n.gate_pre[...] = gate_pre
+    sigma = 1.0 / (1.0 + jnp.exp(-gate_pre))
+    n.grads_own[...] = (n.gated_grad[...] * (gate_pre * sigma)).astype(brain)
+    my_cols = pl.ds(pl.multiple_of(m * cols, LANES), cols)
+
+    def seq_rows(s):
+        return pl.ds(pl.multiple_of(s * length, 16), length)
+
+    g_z = go(
+        [
+            remote(n.grads_own, n.g_all.at[seq_rows(d), my_cols], n.sems_g, k, deep(k))
+            for k in range(1, parts)
+        ]
+    )
+    n.g_all[seq_rows(d), my_cols] = n.grads_own[...]
+    arrive(w_z)
+    w_near = near_gather(n.w_all, n.sems_w)
+    arrive(w_near[:3])
+    w_core = core_gather(n.w_all, n.sems_w)
+    arrive(w_near[3:])
+    arrive(w_core)
+
+    block = n.lo_s.shape[0]
+    pad = n.tiles.shape[0] // block
+
+    def build(i, carry):
+        here = pl.ds(pl.multiple_of(i * block, block), block)
+        local = n.ids_v[here, :]
+        n.lo_s[...] = jnp.where(local < 0, 0, local & (LANES - 1)).astype(floating)
+        n.hi_s[...] = (local >> 7).astype(floating)
+        per_seq = length // block
+        w_t = n.w_all[i // per_seq, :, pl.ds(pl.multiple_of((i % per_seq) * block, block), block)]
+        n.w_s[...] = jnp.transpose(w_t.astype(floating))
+        hot_rows(n.lo_s, n.hi_s, n.w_s, n.tiles, block, pad)
+        for a in range(rows // LANES):
+            n.spread_v[here, a * LANES : (a + 1) * LANES] = n.tiles[
+                pl.ds(a, block, stride=pad), :
+            ].astype(brain)
+        return carry
+
+    blocks = seqs * length // block
+    cuts = [0, blocks // 8, (9 * blocks) // 16, (13 * blocks) // 16, blocks]
+    lax.fori_loop(cuts[0], cuts[1], build, 0)
+    arrive(g_z)
+
+    def whole(s):
+        return n.g_all.at[seq_rows(s)]
+
+    def part(s, h):
+        return n.g_all.at[pl.ds(pl.multiple_of(s * length + h * half, 16), half)]
+
+    g_one = go(
+        [
+            remote(whole(d), whole(d), n.sems_g, 4 + i, at(p))
+            for i, p in enumerate((x_side, y_side, core))
+        ]
+    )
+    lax.fori_loop(cuts[1], cuts[2], build, 0)
+    arrive(g_one[:2])
+    g_two = go(
+        [
+            remote(part(y_side, 0), part(y_side, 0), n.sems_g, 7, at(x_side)),
+            remote(part(x_side, 1), part(x_side, 1), n.sems_g, 8, at(y_side)),
+            remote(whole(x_side), whole(x_side), n.sems_g, 9, at(core)),
+            remote(whole(y_side), whole(y_side), n.sems_g, 10, at(core)),
+        ]
+    )
+    lax.fori_loop(cuts[2], cuts[3], build, 0)
+    arrive(g_two[:2])
+    g_three = go([remote(whole(corner), whole(corner), n.sems_g, 11, at(core))])
+    lax.fori_loop(cuts[3], cuts[4], build, 0)
+
+    table_in.wait()
+    sib_core = core % 2
+
+    def partial_of(seq):
+        return jnp.dot(
+            n.spread_v[seq_rows(seq), :], n.table_v[...], preferred_element_type=floating
+        ).astype(brain)
+
+    to_core = []
+    for c in range(seqs // 2):
+        n.part_sib[c] = partial_of(2 * c + sib_core)
+        to_core += go([remote(n.part_sib.at[c], n.got_core.at[c], n.sems_m, c, at(core))])
+
+    def own_part(c, carry):
+        n.part_own[c] = partial_of(2 * c + d % 2)
+        return carry
+
+    lax.fori_loop(0, seqs // 2, own_part, 0)
+    arrive(to_core)
+
+    def fold(c, carry):
+        n.part_own[c] = (n.part_own[c].astype(floating) + n.got_core[c].astype(floating)).astype(
+            brain
+        )
+        return carry
+
+    lax.fori_loop(0, seqs // 2, fold, 0)
+    upper, lower = pl.ds(0, half), pl.ds(half, half)
+    m_one = go(
+        [
+            remote(n.part_own.at[chip_d, upper], n.got_x.at[0], n.sems_m, 4, at(x_side)),
+            remote(n.part_own.at[chip_d, lower], n.got_y.at[0], n.sems_m, 5, at(y_side)),
+            remote(n.part_own.at[chip_x, upper], n.got_x.at[1], n.sems_m, 6, at(x_side)),
+            remote(n.part_own.at[chip_y, lower], n.got_y.at[1], n.sems_m, 7, at(y_side)),
+        ]
+    )
+
+    arrive(g_two[2:])
+    arrive(g_one[2:])
+    arrive(g_three)
+
+    def answers_of(seq):
+        n.all_s[...] = nt(n.g_all[seq_rows(seq), :], n.table_v[...])
+        local = n.ids_v[seq_rows(seq), :]
+        lo, hi = jnp.where(local < 0, 0, local & (LANES - 1)), local >> 7
+        total = jnp.zeros((length, picks), floating)
+        for a in range(rows // LANES):
+            found = jnp.take_along_axis(
+                n.all_s[:, a * LANES : (a + 1) * LANES], lo, axis=1, mode="promise_in_bounds"
+            )
+            total = jnp.where(hi == a, found, total)
+        return jnp.transpose(total).astype(brain)
+
+    def sib_answers(c, carry):
+        n.ans_sib[c] = answers_of(2 * c + sib_core)
+        return carry
+
+    def own_answers(c, carry):
+        n.ans_own[c] = answers_of(2 * c + d % 2)
+        return carry
+
+    lax.fori_loop(0, seqs // 2, sib_answers, 0)
+    a_core = go([remote(n.ans_sib, n.ans_core, n.sems_a, 0, at(core))])
+    arrive(m_one[:2])
+    n.part_own[chip_y, upper] = (
+        n.part_own[chip_y, upper].astype(floating) + n.got_x[0].astype(floating)
+    ).astype(brain)
+    n.part_own[chip_x, lower] = (
+        n.part_own[chip_x, lower].astype(floating) + n.got_y[0].astype(floating)
+    ).astype(brain)
+    m_two = go(
+        [
+            remote(n.part_own.at[chip_x, lower], n.got_x.at[2], n.sems_m, 8, at(x_side)),
+            remote(n.part_own.at[chip_y, upper], n.got_y.at[2], n.sems_m, 9, at(y_side)),
+        ]
+    )
+    lax.fori_loop(0, seqs // 2, own_answers, 0)
+    arrive(a_core)
+    n.ans_own[...] = (n.ans_own[...].astype(floating) + n.ans_core[...].astype(floating)).astype(
+        brain
+    )
+    a_plane = go(
+        [
+            remote(n.ans_own.at[chip], n.ans_plane.at[i], n.sems_a, 1 + i, at(p))
+            for i, (chip, p) in enumerate(((chip_x, x_side), (chip_y, y_side), (chip_d, corner)))
+        ]
+    )
+    arrive(m_one[2:])
+    arrive(m_two)
+    n.part_own[mine, upper] = (
+        n.part_own[mine, upper].astype(floating)
+        + n.got_x[1].astype(floating)
+        + n.got_y[2].astype(floating)
+    ).astype(brain)
+    n.part_own[mine, lower] = (
+        n.part_own[mine, lower].astype(floating)
+        + n.got_x[2].astype(floating)
+        + n.got_y[1].astype(floating)
+    ).astype(brain)
+
+    def cols_of(k):
+        return pl.ds(pl.multiple_of(z_of[k] * cols, LANES), cols)
+
+    m_z = go(
+        [
+            remote(n.part_own.at[mine, :, cols_of(k)], n.got_z.at[k - 1], n.sems_m, 9 + k, deep(k))
+            for k in range(1, parts)
+        ]
+    )
+
+    tg_block = n.tg_v.shape[1]
+    tg_steps = rows // tg_block
+
+    def tg_out(i):
+        return pltpu.make_async_copy(
+            n.tg_v.at[i % 2],
+            n.table_grad.at[pl.ds(i * tg_block, tg_block)],
+            n.local_sems.at[1 + i % 2],
+        )
+
+    def table_grad_steps(first, last):
+        for i in range(first, last):
+            if i >= 2:
+                tg_out(i - 2).wait()
+            n.tg_v[i % 2] = tn(
+                n.spread_v[:, i * tg_block : (i + 1) * tg_block], n.g_all[...]
+            ).astype(brain)
+            tg_out(i).start()
+
+    tg_cuts = [0, tg_steps // 4, tg_steps // 2, 3 * tg_steps // 4, tg_steps]
+    table_grad_steps(tg_cuts[0], tg_cuts[1])
+    arrive(a_plane)
+    answered = n.ans_own[mine].astype(floating)
+    for k in range(3):
+        answered = answered + n.ans_plane[k].astype(floating)
+    n.ans_own[mine] = answered.astype(brain)
+    a_z = go(
+        [
+            remote(
+                n.ans_own.at[mine, pl.ds(pl.multiple_of(z_of[k] * picks_here, 16), picks_here)],
+                n.ans_z.at[k - 1],
+                n.sems_a,
+                3 + k,
+                deep(k),
+            )
+            for k in range(1, parts)
+        ]
+    )
+    table_grad_steps(tg_cuts[1], tg_cuts[2])
+
+    arrive(a_z)
+    weight_grad = n.ans_own[mine, pick_rows, :].astype(floating)
+    for k in range(parts - 1):
+        weight_grad = weight_grad + n.ans_z[k].astype(floating)
+    weights_t = n.weights_t[...]
+    n.score_grad[...] = weights_t * (
+        weight_grad - jnp.sum(weights_t * weight_grad, axis=0, keepdims=True)
+    )
+    turned = jnp.transpose(n.pick_wide[...].astype(floating))[:picks_here].astype(jnp.int32)
+    n.first_t[...] = (turned // subs).astype(floating)
+    n.second_t[...] = (turned % subs).astype(floating)
+    sub_block = 64
+
+    def gather_subs(i, carry):
+        top = pl.multiple_of(i * sub_block, sub_block)
+        key_at = (lax.broadcasted_iota(jnp.int32, (sub_block, length), 0) + top).astype(floating)
+        for index, out in ((n.first_t, n.first_grad), (n.second_t, n.second_grad)):
+            total = jnp.zeros((sub_block, length), floating)
+            for p in range(picks_here):
+                total = total + jnp.where(
+                    key_at == index[p : p + 1, :], n.score_grad[p : p + 1, :], 0.0
+                )
+            out[pl.ds(top, sub_block), :] = total.astype(brain)
+        return carry
+
+    lax.fori_loop(0, subs // sub_block, gather_subs, 0)
+    query_grad = jnp.concatenate(
+        [
+            tn(n.first_grad[...], n.mem_keys[0, 0]),
+            tn(n.second_grad[...], n.mem_keys[1, 0]),
+        ],
+        axis=1,
+    ).astype(brain)
+    arrive(m_z)
+    memory = n.part_own[mine, :, my_cols].astype(floating)
+    for k in range(parts - 1):
+        memory = memory + n.got_z[k].astype(floating)
+    gate_pre = n.gate_pre[...]
+    sigma = 1.0 / (1.0 + jnp.exp(-gate_pre))
+    gate_grad = (n.gated_grad[...] * memory * (sigma * (1.0 + gate_pre * (1.0 - sigma)))).astype(
+        brain
+    )
+    mem_grads = jnp.concatenate([query_grad, gate_grad], axis=1)
+    low_mem_part = ADAPT_SCALE * nt(mem_grads, padded(n.up_mem[...]))
+    two_part = (
+        nt(query_grad, n.col_weights[3])
+        + nt(gate_grad, n.col_weights[4])
+        + jnp.dot(low_mem_part.astype(brain), padded(down_mem), preferred_element_type=floating)
+    )
+    n.sum_send[1, :, :, :width] = two_part.astype(brain).reshape(parts, quarter, width)
+    n.sum_send[1, :, :, width:] = low_mem_part.astype(brain).reshape(parts, quarter, SIDE)
+    r_two = z_scatter(n.sum_send.at[1], n.sum_got.at[1], n.sems_z.at[2])
+
+    gated = (memory * (gate_pre * sigma)).astype(brain)
+    low_branch_part = nt(gated, padded(row_down[1]))
+    branch_part = jnp.dot(gated, n.row_weights[1], preferred_element_type=floating)
+    branch_part = branch_part + ADAPT_SCALE * jnp.dot(
+        low_branch_part.astype(brain), padded(row_up[1]), preferred_element_type=floating
+    )
+    n.sum_send[2, :, :, :width] = branch_part.astype(brain).reshape(parts, quarter, width)
+    n.sum_send[2, :, :, width:] = low_branch_part.astype(brain).reshape(parts, quarter, SIDE)
+    low_mem = n.low_mem[...]
+    up_mem_grad = ADAPT_SCALE * tn(low_mem, mem_grads)
+    for j in range(2):
+        n.narrow[d, (3 + j) * rank : (4 + j) * rank, :] = up_mem_grad[
+            j * rank : (j + 1) * rank, j * cols : (j + 1) * cols
+        ].astype(brain)
+    n.narrow[d, 6 * rank : 7 * rank, :] = tn(n.low_branch_grad[...], gated)[:rank].astype(brain)
+    table_grad_steps(tg_cuts[2], tg_cuts[3])
+    arrive(r_two)
+    total = total_of(1)
+    resid = n.resid[...]
+    scale_two = lax.rsqrt(jnp.mean(resid * resid, axis=1, keepdims=True) + EPSILON)
+    weighted = gain_two * total[:, :width]
+    resid_grad = (
+        n.cotangent[my_rows, :].astype(floating)
+        + scale_two * weighted
+        - resid * scale_two**3 * jnp.mean(resid * weighted, axis=1, keepdims=True)
+    )
+    n.resid_grad[...] = resid_grad
+    n.gath_grad[m, :, :width] = resid_grad.astype(brain)
+    n.gath_grad[m, :, width:] = total[:, width:].astype(brain)
+    q_grad = z_gather(n.gath_grad, n.sems_z.at[3])
+    table_grad_steps(tg_cuts[3], tg_cuts[4])
+    arrive(q_grad)
+    r_branch = z_scatter(n.sum_send.at[2], n.sum_got.at[2], n.sems_z.at[4])
+
+    branch_grad = n.gath_grad[:, :, :width].reshape(length, width)
+    low_out_grad = (ADAPT_SCALE * nt(branch_grad, padded(row_up[0]))).astype(brain)
+    att_out_grad = (
+        nt(branch_grad, n.row_weights[0])
+        + jnp.dot(low_out_grad, padded(row_down[0]), preferred_element_type=floating)
+    ).astype(brain)
+    for pair in range(heads // sides):
+        query2, key2, value2 = (pair_of(w, pair) for w in range(3))
+        out2 = att_out_grad[:, pair * LANES : (pair + 1) * LANES]
+        grads2 = [jnp.zeros((length, LANES), floating)] * 3
+        for side in range(sides):
+            own = lane // HEAD_DIM == side
+            probs = n.probs[pair * sides + side]
+            prob_grad = nt(jnp.where(own, out2, brain(0)), value2)
+            logit_grad = (
+                probs * (prob_grad - jnp.sum(probs * prob_grad, axis=1, keepdims=True))
+            ).astype(brain)
+            made = (
+                0.125 * jnp.dot(logit_grad, key2, preferred_element_type=floating),
+                0.125 * tn(logit_grad, query2),
+                tn(probs.astype(brain), out2),
+            )
+            grads2 = [jnp.where(own, new, old) for new, old in zip(made, grads2)]
+        for w in range(3):
+            first = w * cols + pair * LANES
+            n.proj_grad[:, first : first + LANES] = grads2[w].astype(brain)
+    proj_grad = n.proj_grad[...]
+    low_att_part = ADAPT_SCALE * nt(proj_grad, padded(n.up_att[...]))
+    one_part = jnp.dot(low_att_part.astype(brain), padded(down_att), preferred_element_type=floating)
+    for j in range(3):
+        one_part = one_part + nt(n.proj_grad[:, j * cols : (j + 1) * cols], n.col_weights[j])
+    n.sum_send[3, :, :, :width] = one_part.astype(brain).reshape(parts, quarter, width)
+    n.sum_send[3, :, :, width:] = low_att_part.astype(brain).reshape(parts, quarter, SIDE)
+    r_one = z_scatter(n.sum_send.at[3], n.sum_got.at[3], n.sems_z.at[5])
+
+    up_att_grad = ADAPT_SCALE * tn(n.low_att[...], proj_grad)
+    for j in range(3):
+        n.narrow[d, j * rank : (j + 1) * rank, :] = up_att_grad[
+            j * rank : (j + 1) * rank, j * cols : (j + 1) * cols
+        ].astype(brain)
+    n.narrow[d, 5 * rank : 6 * rank, :] = tn(low_out_grad, n.att_out[...])[:rank].astype(brain)
+    low_mem_grad = n.gath_grad[:, :, width:].reshape(length, SIDE)
+    normed_two = n.gath_two[:, :, :width].reshape(length, width)
+    n.early[d, : 2 * rank, :] = tn(low_mem_grad, normed_two)[: 2 * rank].astype(brain)
+    low_out = n.gath_two[:, :, width:].reshape(length, SIDE)
+    n.early[d, 2 * rank :, :] = (ADAPT_SCALE * tn(low_out, branch_grad))[:rank].astype(brain)
+    n_near = near_gather(n.narrow, n.sems_b.at[0])
+    e_near = near_gather(n.early, n.sems_b.at[1])
+    arrive(r_branch)
+    total = total_of(2)
+    n.gath_out[m] = (n.resid[...] + total[:, :width]).astype(brain)
+    n.gath_low[0, m] = total[:, width:].astype(brain)
+    q_low = z_gather(n.gath_low.at[0], n.sems_z.at[6])
+    arrive(r_one)
+    total = total_of(3)
+    n.gath_low[1, m] = total[:, width:].astype(brain)
+    q_low_att = z_gather(n.gath_low.at[1], n.sems_z.at[7])
+    weighted = gain_one * total[:, :width]
+    inputs = n.block_in[my_rows, :].astype(floating)
+    scale_one = lax.rsqrt(jnp.mean(inputs * inputs, axis=1, keepdims=True) + EPSILON)
+    n.gath_in[m] = (
+        n.resid_grad[...]
+        + scale_one * weighted
+        - inputs * scale_one**3 * jnp.mean(inputs * weighted, axis=1, keepdims=True)
+    ).astype(brain)
+    q_in = z_gather(n.gath_in, n.sems_z.at[8])
+    q_out = z_gather(n.gath_out, n.sems_z.at[9])
+    arrive(n_near[:3])
+    arrive(e_near[:3])
+    n_core = core_gather(n.narrow, n.sems_b.at[0])
+    e_core = core_gather(n.early, n.sems_b.at[1])
+    arrive(q_low)
+    low_branch = n.gath_low[0].reshape(length, SIDE)
+    n.late[d, 3 * rank :, :] = (ADAPT_SCALE * tn(low_branch, n.cotangent[...]))[:rank].astype(brain)
+    arrive(q_low_att)
+    low_att_grad = n.gath_low[1].reshape(length, SIDE)
+    n.late[d, : 3 * rank, :] = tn(low_att_grad, n.normed_one[...])[: 3 * rank].astype(brain)
+    l_near = near_gather(n.late, n.sems_b.at[2])
+    arrive(n_near[3:] + e_near[3:] + n_core + e_core)
+    arrive(l_near[:3])
+    l_core = core_gather(n.late, n.sems_b.at[2])
+    arrive(l_near[3:])
+    arrive(l_core)
+
+    def place(a, carry):
+        wide_late = jnp.zeros(n.late.shape[1:], brain)
+        wide_early = jnp.zeros(n.early.shape[1:], brain)
+        thin = jnp.zeros(n.narrow.shape[1:], brain)
+        for s in range(seqs):
+            is_it = (n.who[s, 0:1, 0:1] == a).astype(floating).astype(brain)
+            wide_late = wide_late + n.late[s] * is_it
+            wide_early = wide_early + n.early[s] * is_it
+            thin = thin + n.narrow[s] * is_it
+        for j in range(3):
+            n.col_down_grad[j, a] = wide_late[j * rank : (j + 1) * rank]
+            n.col_up_grad[j, a] = thin[j * rank : (j + 1) * rank]
+        for j in range(2):
+            n.col_down_grad[3 + j, a] = wide_early[j * rank : (j + 1) * rank]
+            n.col_up_grad[3 + j, a] = thin[(3 + j) * rank : (4 + j) * rank]
+            n.row_down_grad[j, a] = thin[(5 + j) * rank : (6 + j) * rank]
+        n.row_up_grad[0, a] = wide_early[2 * rank :]
+        n.row_up_grad[1, a] = wide_late[3 * rank :]
+        return carry
+
+    lax.fori_loop(0, n.col_down.shape[1], place, 0)
+    arrive(q_in)
+    n.input_grad[...] = n.gath_in[...].reshape(length, width)
+    arrive(q_out)
+    n.block_out[...] = n.gath_out[...].reshape(length, width)
+    for i in range(max(tg_steps - 2, 0), tg_steps):
+        tg_out(i).wait()
+    for c in sent:
+        c.wait_send()
+
+
+def whole_block(args, seqs, parts):
+    floating, brain, whole = jnp.float32, jnp.bfloat16, jnp.int32
+    given = Refs()
+    given.__dict__.update(args)
+    length, width = given.block_in.shape
+    rows = given.table.shape[0]
+    cols, quarter = width // parts, length // parts
+    picks_here = given.pick_ids.shape[1]
+    picks = picks_here * parts
+    rank = given.col_down.shape[2]
+    subs = given.mem_keys.shape[2]
+    tokens = seqs * length
+    block, tg_block = 128, 256
+    pad = max(rows // LANES, 16)
+    vmem = pl.BlockSpec(memory_space=pltpu.VMEM)
+    anywhere = pl.BlockSpec(memory_space=pl.ANY)
+    places = dict(adapter_ids=pl.BlockSpec(memory_space=pltpu.SMEM), table=anywhere)
+    outs = dict(
+        block_out=((length, width), brain),
+        input_grad=((length, width), brain),
+        table_grad=((rows, width), brain),
+        col_down_grad=(given.col_down.shape, brain),
+        col_up_grad=(given.col_up.shape, brain),
+        row_down_grad=(given.row_down.shape, brain),
+        row_up_grad=(given.row_up.shape, brain),
+    )
+    chips = seqs // 2
+    scratch = dict(
+        table_v=((rows, width), brain),
+        pick_wide=((length, LANES), whole),
+        picks_own=((picks_here, length), whole),
+        ids_t=((seqs, picks, length), whole),
+        ids_v=((tokens, picks), whole),
+        who=((seqs, 8, LANES), whole),
+        normed_one=((length, width), brain),
+        up_att=((3 * rank, 3 * cols), brain),
+        up_mem=((2 * rank, 2 * cols), brain),
+        low_att=((length, 3 * rank), brain),
+        low_mem=((length, 2 * rank), brain),
+        proj=((length, 3 * cols), brain),
+        proj_grad=((length, 3 * cols), brain),
+        probs=((cols // HEAD_DIM, length, length), floating),
+        att_out=((length, cols), brain),
+        sum_send=((4, parts, quarter, width + SIDE), brain),
+        sum_got=((4, parts - 1, quarter, width + SIDE), brain),
+        low_branch_grad=((length, SIDE), brain),
+        gated_grad=((length, cols), floating),
+        resid=((quarter, width), floating),
+        resid_grad=((quarter, width), floating),
+        gath_two=((parts, quarter, width + SIDE), brain),
+        gath_grad=((parts, quarter, width + SIDE), brain),
+        gath_out=((parts, quarter, width), brain),
+        gath_in=((parts, quarter, width), brain),
+        gath_low=((2, parts, quarter, SIDE), brain),
+        weights_t=((picks_here, length), floating),
+        weights_own=((picks_here, length), brain),
+        w_all=((seqs, picks, length), brain),
+        gate_pre=((length, cols), floating),
+        grads_own=((length, cols), brain),
+        g_all=((tokens, width), brain),
+        spread_v=((tokens, rows), brain),
+        tiles=((block * pad, LANES), floating),
+        lo_s=((block, picks), floating),
+        hi_s=((block, picks), floating),
+        w_s=((block, picks), floating),
+        part_own=((chips, length, width), brain),
+        part_sib=((chips, length, width), brain),
+        got_core=((chips, length, width), brain),
+        got_x=((3, length // 2, width), brain),
+        got_y=((3, length // 2, width), brain),
+        got_z=((parts - 1, length, cols), brain),
+        ans_own=((chips, picks, length), brain),
+        ans_sib=((chips, picks, length), brain),
+        ans_core=((chips, picks, length), brain),
+        ans_plane=((3, picks, length), brain),
+        ans_z=((parts - 1, picks_here, length), brain),
+        all_s=((length, rows), floating),
+        tg_v=((2, tg_block, width), brain),
+        score_grad=((picks_here, length), floating),
+        first_t=((picks_here, length), floating),
+        second_t=((picks_here, length), floating),
+        first_grad=((subs, length), brain),
+        second_grad=((subs, length), brain),
+        narrow=((seqs, 7 * rank, cols), brain),
+        early=((seqs, 3 * rank, width), brain),
+        late=((seqs, 4 * rank, width), brain),
+    )
+    semaphores = dict(
+        local_sems=(3,),
+        sems_i=(2, 12),
+        sems_w=(2, 12),
+        sems_g=(2, 12),
+        sems_m=(2, 14),
+        sems_a=(2, 8),
+        sems_z=(10, 2, 4),
+        sems_b=(3, 2, 12),
+    )
+    names = [*args, *outs, *scratch, *semaphores]
+    return pl.pallas_call(
+        functools.partial(block_kernel, names, seqs, parts),
+        in_specs=[places.get(name, vmem) for name in args],
+        out_specs=[anywhere if name == "table_grad" else vmem for name in outs],
+        out_shape=[jax.ShapeDtypeStruct(*made) for made in outs.values()],
+        scratch_shapes=[pltpu.VMEM(*made) for made in scratch.values()]
+        + [pltpu.SemaphoreType.DMA(shape) for shape in semaphores.values()],
+        compiler_params=pltpu.CompilerParams(
+            collective_id=0, has_side_effects=True, vmem_limit_bytes=62 * 2**20
+        ),
+        name="whole_block",
+    )(*args.values())
 
 
 def pick_scores(picks, first, second, sub_count):
@@ -421,6 +1254,42 @@
     )
 
 
+def fused(
+    block_in,
+    cotangent,
+    norm_gains,
+    col_weights,
+    row_weights,
+    mem_keys,
+    value_table,
+    col_down,
+    col_up,
+    row_down,
+    row_up,
+    segment_ids,
+    adapter_ids,
+    pick_ids,
+):
+    args = dict(
+        block_in=block_in,
+        cotangent=cotangent,
+        norm_gains=norm_gains,
+        col_weights=col_weights,
+        row_weights=row_weights,
+        mem_keys=mem_keys,
+        table=value_table,
+        col_down=col_down,
+        col_up=col_up,
+        row_down=row_down,
+        row_up=row_up,
+        segment_ids=segment_ids,
+        adapter_ids=adapter_ids,
+        pick_ids=pick_ids[:, 0, :],
+    )
+    outs = whole_block(args, lax.axis_size("dp"), lax.axis_size("mp"))
+    return (outs[0], *(out.astype(jnp.float32) for out in outs[1:]))
+
+
 def solution(mesh):
     in_specs = (
         P("dp", None),
@@ -447,6 +1316,7 @@
         P(None, None, None, "mp"),
         P(),
     )
+    step = fused if mesh.shape["dp"] == 8 else per_device
     return jax.shard_map(
-        per_device, mesh=mesh, in_specs=in_specs, out_specs=out_specs, check_vma=False
-    )
+        step, mesh=mesh, in_specs=in_specs, out_specs=out_specs, check_vma=False
+    )

time: 615 us -> 230 us (0.37)
  waiting for transfers between devices: 280 us -> 0 us
  Pallas kernels: 53.5 us -> 214 us
  blocking collectives: 114 us -> 0 us
  matrix products: 93.5 us -> 0 us
  other arithmetic: 37.4 us -> 12.4 us
  between operations: 17.1 us -> 1.31 us
  local copies, waits for them, and re-layouts: 16.9 us -> 2.33 us
    pallas_call x2 -> x1, Pallas kernels: 53.5 us -> 214 us  [whole_block(): pl.pallas_call(functools.partial(block_kernel, names, seqs, parts), in_sp...]
    psum x4 -> x0, waiting for transfers between devices: 131 us -> none  [the longest x1 61.7 us: per_device(): lax.psum(down_cols_all.astype(jnp.bfloat16), 'dp').astype(jnp.float32)]
    reduce_scatter x3 -> x0, waiting for transfers between devices: 98.2 us -> none  [the longest x1 49.7 us: per_device(): mem_cols = lax.psum_scatter(partial, 'dp', scatter_dimension=0, tiled=True)]
    dot_general x49 -> x0, matrix products: 93.5 us -> none  [the longest x13 32 us: matmul(): return jnp.dot(left, right, preferred_element_type=jnp.float32)]
    all_gather x4 -> x0, blocking collectives: 58.2 us -> none  [the longest x1 16.6 us: per_device(): lax.all_gather(mem_grad_cols, 'mp', axis=1, tiled=True)]
    psum x3 -> x0, blocking collectives: 55.4 us -> none  [the longest x1 19.6 us: per_device(): att_sum, low_sum = lax.psum((att_part, low_part), 'mp')]
    all_gather x2 -> x0, waiting for transfers between devices: 34.6 us -> none  [the longest x1 34.6 us: per_device(): lax.all_gather(lax.all_gather(mem_grad_cols, 'mp', axis=1, tiled=True), '...]
    unnamed x11 -> x0, waiting for transfers between devices: 16.1 us -> none
  transfers between devices with their start and end apart: 10 -> 0, of which waited for: 9 -> 0; matrix products, arithmetic and copies ran while one was open for 11% -> 0% of each run, Pallas kernels for 0% -> 0%
where the time goes in v3:
time: 230 us
  Pallas kernels  214 us (93%)
  other arithmetic  12.4 us (5%)
  local copies, waits for them, and re-layouts  2.33 us (1%)
    pallas_call x1, Pallas kernels, whole_block(): pl.pallas_call(functools.partial(block_kernel, names, seqs, parts), in_sp...  214 us
    convert_element_type x6, other arithmetic, fused(): return (outs[0], *(out.astype(jnp.float32) for out in outs[1:]))  12.4 us

profile of v3, /device:TPU:0, one launch (start us, length us, event | category | flops | bytes accessed | tf_op | source)
XLA Modules:
  0.0 230.0 jit_solution(16624118227748282897)
XLA Ops:
  0.6 1.5 copy.21
  2.8 214.0 %whole_block.1 = (bf16[256,1024]{1,0:T(8,128)(2,1)}, bf16[256,1024]{1,0:T(8,128)(2,1)}, bf16[2048,1024]{1,0:T(8,128)(2,1)}, bf16[5,8,16,1024]{3,2,1,0:T(8,128)(2...) custom-call(bf16[256,1024]{1,0:T(8,128)(2,1)} %refs_0_.1, ...), custom_call_target="tpu_custom_call" | custom-call | tf_op jit(solution)/shard_map/whole_block/pallas_call | solution.py:971
  216.8 0.0 copy-start
  216.9 6.7 %convert_element_type.19 = f32[2048,1024]{1,0:T(8,128)} convert(bf16[2048,1024]{1,0:T(8,128)(2,1)} %get-tuple-element.16) | non-fusion elementwise | flops 2097152 | bytes 12582912 | tf_op jit(solution)/shard_map/convert_element_type | solution.py:1290
  223.6 0.0 copy-start.2
  223.6 0.0 copy-done
  223.6 0.0 copy-start.1
  223.6 0.0 copy-start.4
  223.6 1.8 convert_element_type.20
  225.4 0.0 copy-start.5
  225.4 0.0 copy-start.3
  225.4 0.0 copy-done.2
  225.4 1.1 convert_element_type.18
  226.5 0.0 copy-done.1
  226.5 1.1 convert_element_type.23
  227.6 0.0 copy-done.4
  227.6 0.9 convert_element_type.21
  228.5 0.0 copy-done.5
  228.5 0.7 convert_element_type.22
  229.2 0.0 copy-done.3
  229.2 0.8 copy.24
Async XLA Ops:
  216.8 6.8 %copy-start = (bf16[5,8,16,1024]{3,2,1,0:T(8,128)(2,1)S(1)}, bf16[5,8,16,1024]{3,2,1,0:T(8,128)(2,1)}, u32[]{:S(2)}) copy-start(bf16[5,8,16,1024]{3,2,1,0:T(8,128)(2,1)} %get-tuple-element.17) | copy-start | bytes 3932164
  223.6 1.8 copy-start.2
  223.6 2.9 %copy-start.1 = (bf16[2,8,16,1024]{3,2,1,0:T(8,128)(2,1)S(1)}, bf16[2,8,16,1024]{3,2,1,0:T(8,128)(2,1)}, u32[]{:S(2)}) copy-start(bf16[2,8,16,1024]{3,2,1,0:T(8,128)(2,1)} %get-tuple-element.20) | copy-start | bytes 1572868
  223.6 4.0 %copy-start.4 = (bf16[5,8,16,256]{3,2,1,0:T(8,128)(2,1)S(1)}, bf16[5,8,16,256]{3,2,1,0:T(8,128)(2,1)}, u32[]{:S(2)}) copy-start(bf16[5,8,16,256]{3,2,1,0:T(8,128)(2,1)} %get-tuple-element.18) | copy-start | bytes 983044
  225.4 3.1 %copy-start.5 = (bf16[2,8,16,256]{3,2,1,0:T(8,128)(2,1)S(1)}, bf16[2,8,16,256]{3,2,1,0:T(8,128)(2,1)}, u32[]{:S(2)}) copy-start(bf16[2,8,16,256]{3,2,1,0:T(8,128)(2,1)} %get-tuple-element.19) | copy-start | bytes 393220
  225.4 3.8 %copy-start.3 = (bf16[256,1024]{1,0:T(8,128)(2,1)S(1)}, bf16[256,1024]{1,0:T(8,128)(2,1)}, u32[]{:S(2)}) copy-start(bf16[256,1024]{1,0:T(8,128)(2,1)} %get-tuple-element.28) | copy-start | bytes 1572868
